TPU v7x, 32 devices: a whole 2x2x4 slice. The times are simulated.
32 devices in a mesh: space: 8 (over y, x, core), help: 4 (over z).
Axes of the slice: x: 2, y: 2, z: 4, core: 2. Of those that a mesh axis runs over, the one named last changes fastest.
Arguments:
- solution: float32 [9, 4096, 512], P(None, ('space', 'help')), may hold values from -6 to 6
- material: float32 [3, 4096, 512], P(None, ('space', 'help')), may hold values from 0.5 to 2
- neighbours: int32 [6, 4096], P(None, ('space', 'help')), may hold values from 0 to 4095, as said below
- refine_count: int32 [8, 4], P('space', 'help'), may hold values from 1 to 64, 128 in all within a row
Outputs:
- evolved: float32 [9, 4096, 512], P(None, ('space', 'help'))
Inputs may be any that keep to these rules, and one draw needn't show every extreme that they name: The neighbours across y and z faces lie on the same device; across x+ on the device next along space (index + 1, wrapping) with the same help index, across x- on the previous one. Neighbours are mutual: the x+ neighbour's x- neighbour is the cell itself, likewise for y and z. `refine_count`: A device's cells whose index within the device is under its count are refined; the counts of one help group sum to 128.
All inputs are finite; a program needn't handle non-finite values.
Results may differ from a plain program's by a relative error of at most 0.0001.
Values sent between devices are 32-bit elements; how exact they have to be, the bound alone decides.
No kernel may reach another device: no remote copies, remote signals or barrier semaphores. Data moves between devices by JAX's collectives and lax.ppermute only.
A program may use at most 128 MiB of HBM per device.

v0:
```python
import math

import jax
import jax.numpy as jnp
import numpy as np
from jax import lax
from jax.sharding import PartitionSpec as P

P_SIZE = 8
ORD = 8
ORD_LOW = 2
BLK = 16
REF_MAX = 64


along_x = (6, 7, 8, 0, 3, 5)
along_y = (6, 7, 8, 3, 1, 4)
along_z = (6, 7, 8, 5, 4, 2)
time_step = 0.5
lift_gain = 0.5
highest = lax.Precision.HIGHEST


def shifted(value, axis, by):
    peers = lax.axis_size(axis)
    return lax.ppermute(value, axis, [(i, (i + by) % peers) for i in range(peers)])


def cheb_table(node_count):
    intervals = node_count - 1
    places = np.arange(node_count)
    points = np.cos(np.pi * places / intervals)
    weights = np.where((places == 0) | (places == intervals), 2.0, 1.0)
    scaled = weights * (-1.0) ** places
    differ = points[:, None] - points[None, :] + np.eye(node_count)
    matrix = np.outer(scaled, 1.0 / scaled) / differ
    matrix = matrix - np.eye(node_count) * np.sum(matrix, axis=1)[:, None]
    return matrix / (node_count * node_count / 4.0)


def taylor_weight(degree):
    return time_step ** (degree + 1) / math.factorial(degree + 1)


def derive_all(values, slope_table):
    fields, cell_count = (values.shape[0], values.shape[1])
    volume = values.reshape(fields, cell_count, P_SIZE, P_SIZE, P_SIZE)
    patterns = ("ij,vcjbe->vcibe", "ij,vcaje->vcaie", "ij,vcabj->vcabi")
    return [
        jnp.einsum(pattern, slope_table, volume, precision=highest).reshape(
            fields, cell_count, P_SIZE * P_SIZE * P_SIZE
        )
        for pattern in patterns
    ]


def elastic(slope_x, slope_y, slope_z, material):
    density, lame_first, shear_modulus = (material[0], material[1], material[2])
    diverge = slope_x[0] + slope_y[1] + slope_z[2]
    normal_x = lame_first * diverge + 2.0 * shear_modulus * slope_x[0]
    normal_y = lame_first * diverge + 2.0 * shear_modulus * slope_y[1]
    normal_z = lame_first * diverge + 2.0 * shear_modulus * slope_z[2]
    shear_xy = shear_modulus * (slope_y[0] + slope_x[1])
    shear_yz = shear_modulus * (slope_z[1] + slope_y[2])
    shear_xz = shear_modulus * (slope_z[0] + slope_x[2])
    speed_x = (slope_x[3] + slope_y[3] + slope_z[3]) / density
    speed_y = (slope_x[4] + slope_y[4] + slope_z[4]) / density
    speed_z = (slope_x[5] + slope_y[5] + slope_z[5]) / density
    return jnp.stack(
        [normal_x, normal_y, normal_z, shear_xy, shear_yz, shear_xz, speed_x, speed_y, speed_z]
    )


def operate(values, material, slope_table):
    picks = (along_x, along_y, along_z)
    derived = derive_all(values, slope_table)
    slopes = [[derived[direction][member] for member in picks[direction]] for direction in range(3)]
    return elastic(slopes[0], slopes[1], slopes[2], material)


def face_trace(values, direction, place):
    shape = values.shape[:-1]
    volume = values.reshape(shape + (P_SIZE, P_SIZE, P_SIZE))
    picked = lax.index_in_dim(volume, place, axis=len(shape) + direction, keepdims=False)
    return picked.reshape(shape + (P_SIZE * P_SIZE,))


def add_trace(volume, correction, direction, place):
    fields, cell_count = (volume.shape[0], volume.shape[1])
    chosen = (slice(None), slice(None)) + (slice(None),) * direction + (place,)
    return volume.at[chosen].add(correction.reshape(fields, cell_count, P_SIZE, P_SIZE))


def face_flux(own_trace, far_trace, own_speed, far_speed, medium, direction, normal_sign):
    picks = (along_x, along_y, along_z)
    difference = far_trace - own_trace
    top_speed = jnp.maximum(own_speed, far_speed)
    nothing = (0.0,) * 6
    slopes = [nothing, nothing, nothing]
    slopes[direction] = tuple((difference[member] for member in picks[direction]))
    normal = elastic(slopes[0], slopes[1], slopes[2], medium)
    return lift_gain * (0.5 * normal_sign * normal + 0.5 * top_speed[None] * difference)


def continue_terms(current, material, slope_table):
    extra_part = jnp.zeros_like(current)
    for degree in range(ORD_LOW, ORD):
        current = operate(current, material, slope_table)
        extra_part = extra_part + taylor_weight(degree) * current
    return extra_part


def run_blocks(last_term, last_medium, active, slope_table):
    rounds = (active + BLK - 1) // BLK

    def run_block(block_index, buffer):
        offset = block_index * BLK
        portion = lax.dynamic_slice_in_dim(last_term, offset, BLK, 1)
        medium = lax.dynamic_slice_in_dim(last_medium, offset, BLK, 1)
        return lax.dynamic_update_slice_in_dim(
            buffer, continue_terms(portion, medium, slope_table), offset, 1
        )

    return lax.fori_loop(jnp.int32(0), rounds, run_block, jnp.zeros_like(last_term))


def offload(last_term, last_medium, active, slope_table):
    helpers = lax.axis_size("help")
    position = lax.axis_index("help")
    slot_count = last_term.shape[1]
    node_total = last_term.shape[2]
    per_helper = slot_count // helpers
    outgoing = last_term.reshape(9, per_helper, helpers, node_total)
    outgoing_medium = last_medium.reshape(3, per_helper, helpers, node_total)
    counts_out = jnp.broadcast_to(active.astype(jnp.float32), (1, 1, helpers, 1))
    got_term, got_medium, got_counts = (
        lax.all_to_all(outgoing, "help", split_axis=2, concat_axis=2, tiled=True),
        lax.all_to_all(outgoing_medium, "help", split_axis=2, concat_axis=2, tiled=True),
        lax.all_to_all(counts_out, "help", split_axis=2, concat_axis=2, tiled=True),
    )
    sources = got_counts.reshape(helpers).astype(jnp.int32)
    slot_rank = jnp.arange(per_helper, dtype=jnp.int32)[:, None] * helpers + position
    alive_slot = (slot_rank < sources[None, :]).reshape(slot_count)
    packing = jnp.argsort(jnp.where(alive_slot, 0, 1).astype(jnp.int32), stable=True)
    alive_total = jnp.sum(alive_slot.astype(jnp.int32))
    packed = jnp.take(got_term.reshape(9, slot_count, node_total), packing, axis=1)
    packed_medium = jnp.take(got_medium.reshape(3, slot_count, node_total), packing, axis=1)
    computed = run_blocks(packed, packed_medium, alive_total, slope_table)
    unpacked = jnp.take(computed, jnp.argsort(packing), axis=1)
    returned = lax.all_to_all(
        unpacked.reshape(9, per_helper, helpers, node_total),
        "help",
        split_axis=2,
        concat_axis=2,
        tiled=True,
    )
    return returned.reshape(9, slot_count, node_total)


def rim_pack(face_values, face_speeds):
    return jnp.concatenate([face_values, face_speeds[None]], axis=0).reshape(10, -1)


def split_rims(rims, cell_count, square):
    shaped = rims.reshape(10, cell_count, square)
    return (shaped[:9], shaped[9])


def on_device(solution, material, neighbours, refine_count):
    slope_table = jnp.asarray(cheb_table(P_SIZE), jnp.float32)
    square = P_SIZE * P_SIZE
    cell_count = solution.shape[1]
    refined_total = refine_count[0, 0]
    current = solution
    base_part = time_step * solution
    current = operate(current, material, slope_table)
    base_part = base_part + taylor_weight(1) * current
    wave_speed = jnp.sqrt((material[1] + 2.0 * material[2]) / material[0])
    last_term = current[:, :REF_MAX]
    last_medium = material[:, :REF_MAX]
    extra_part = offload(last_term, last_medium, refined_total, slope_table)
    refined = jnp.arange(REF_MAX, dtype=jnp.int32) < refined_total
    kept = jnp.where(refined[None, :, None], extra_part, 0.0)
    integral = jnp.concatenate([base_part[:, :REF_MAX] + kept, base_part[:, REF_MAX:]], axis=1)
    sent_after = shifted(
        rim_pack(face_trace(integral, 0, P_SIZE - 1), face_trace(wave_speed, 0, P_SIZE - 1)),
        "space",
        -1,
    )
    sent_before = shifted(
        rim_pack(face_trace(integral, 0, 0), face_trace(wave_speed, 0, 0)), "space", 1
    )
    after_values, after_speeds = split_rims(sent_after, cell_count, square)
    before_values, before_speeds = split_rims(sent_before, cell_count, square)
    local_ids = neighbours % cell_count
    result = solution + operate(integral, material, slope_table)
    volume = result.reshape(9, cell_count, P_SIZE, P_SIZE, P_SIZE)
    for slot in range(6):
        direction = slot // 2
        upper_side = slot % 2 == 1
        own_place = 0 if upper_side else P_SIZE - 1
        far_place = P_SIZE - 1 if upper_side else 0
        normal_sign = 1.0 if upper_side else -1.0
        target = local_ids[slot]
        if slot == 0:
            chosen_values, chosen_speeds = (before_values, before_speeds)
        elif slot == 1:
            chosen_values, chosen_speeds = (after_values, after_speeds)
        else:
            chosen_values = face_trace(integral, direction, far_place)
            chosen_speeds = face_trace(wave_speed, direction, far_place)
        correction = face_flux(
            face_trace(integral, direction, own_place),
            jnp.take(chosen_values, target, axis=1),
            face_trace(wave_speed, direction, own_place),
            jnp.take(chosen_speeds, target, axis=0),
            face_trace(material, direction, own_place),
            direction,
            normal_sign,
        )
        volume = add_trace(volume, correction, direction, own_place)
    return volume.reshape(9, cell_count, P_SIZE * P_SIZE * P_SIZE)


def solution(mesh):
    in_specs = (
        P(None, ("space", "help"), None),
        P(None, ("space", "help"), None),
        P(None, ("space", "help")),
        P("space", "help"),
    )
    out_specs = P(None, ("space", "help"), None)
    return jax.shard_map(
        on_device, mesh=mesh, in_specs=in_specs, out_specs=out_specs, check_vma=False
    )
```

profile of v0, /device:TPU:0, one launch (start us, length us, event | category | flops | bytes accessed | tf_op | source)
XLA Modules:
  0.0 673.4 jit_solution(3938171398700637495)
XLA Ops:
  1.2 6.3 all-to-all-start
  16.5 3.6 fusion.73
  20.1 4.7 fusion.77
  34.3 5.1 all-to-all-start.1
  50.6 4.0 all-to-all-start.2
  63.9 18.1 %all-to-all-done.2 = f32[9,16,4,512]{3,1,0,2:T(8,128)S(1)} async-done(((f32[9,16,4,512]{3,1,0,2:T(8,128)}), f32[9,16,4,512]{3,1,0,2:T(8,128)S(1)}, u32[]{:S(2)}, u32[]{:S(2)}) %all-to-all-start.2) | async-done | bytes 1179680 | tf_op jit(solution)/shard_map/all_to_all | solution.py:137
  89.1 366.9 %while.17 = (s32[]{:T(128)}, f32[9,64,512]{2,1,0:T(8,128)}, s32[]{:T(128)}, f32[3,64,512]{2,0,1:T(4,128)S(1)}, f32[9,64,512]{2,0,1:T(8,128)}, /*index=5*/s32[]{:...) while((s32[]{:T(128)}, f32[9,64,512]{2,1,0:T(8,128)}, ...), condition=%wide.region_3.5_spmd.clone, body=%wide.region_2.4_spmd.sunk.clone.sunk | while | flops 129490952 | bytes 78976304 | solution.py:124
  93.7 3.6 fusion.276
  174.3 3.7 fusion.300
  193.4 3.7 fusion.306
  214.6 3.6 fusion.276
  295.0 3.8 fusion.300
  314.1 3.9 fusion.306
  335.3 3.6 fusion.276
  415.7 3.9 fusion.300
  435.0 3.7 fusion.306
  463.7 4.3 all-to-all-start.3
  473.4 22.7 %all-to-all-done.3 = f32[9,16,4,512]{3,1,0,2:T(8,128)} async-done(((f32[9,16,4,512]{3,1,0,2:T(8,128)}), f32[9,16,4,512]{3,1,0,2:T(8,128)}, u32[]{:S(2)}, u32[]{:S(2)}) %all-to-all-start.3) | async-done | bytes 1179680 | tf_op jit(solution)/shard_map/all_to_all | solution.py:150
  504.7 4.0 slice_add_fusion.36
  517.2 3.6 fusion.80
  595.7 9.2 %concatenate.40 = f32[9,8192]{1,0:T(8,128)} reshape(f32[9,128,1,8,8]{4,3,1,0,2:T(8,128)} %copy.1968) | data formatting | bytes 589824 | tf_op jit(solution)/shard_map/concatenate | solution.py:161
  611.3 9.2 %concatenate.37 = f32[9,8192]{1,0:T(8,128)} reshape(f32[9,128,1,8,8]{4,3,1,0,2:T(8,128)} %copy.1962) | data formatting | bytes 589824 | tf_op jit(solution)/shard_map/concatenate | solution.py:161
  659.2 5.7 scatter-add.26
  665.3 5.7 scatter-add.29
  (1207 shorter events, 521.0 us)
Async XLA Ops:
  1.2 33.1 %all-to-all-start = ((f32[1,1,4,1]{3,1,0,2:T(1,128)}), f32[1,1,4,1]{3,1,0,2:T(1,128)S(1)}, u32[]{:S(2)}, u32[]{:S(2)}) async-start(f32[1,1,4,1]{3,1,0,2:T(1,128)} %broadcast_in_dim.76), calls=%async_computation | async-start | bytes 4096 | tf_op jit(solution)/shard_map/all_to_all | solution.py:139
  10.7 22.4 %copy-start.10 = (f32[3,128,512]{1,2,0:T(8,128)}, f32[3,128,512]{1,2,0:T(8,128)S(1)}, u32[]{:S(2)}) copy-start(f32[3,128,512]{1,2,0:T(8,128)S(1)} %copy.1912) | copy-start | bytes 2359300
  34.2 8.2 %copy-start.49 = (f32[1,128,512]{1,2,0:T(8,128)S(1)}, f32[1,128,512]{1,2,0:T(8,128)}, u32[]{:S(2)}) copy-start(f32[1,128,512]{1,2,0:T(8,128)} %get-tuple-element.420) | copy-start | bytes 786436
  34.3 16.3 %all-to-all-start.1 = ((f32[3,16,4,512]{3,1,0,2:T(8,128)}), f32[3,16,4,512]{3,1,0,2:T(8,128)S(1)}, u32[]{:S(2)}, u32[]{:S(2)}) async-start(f32[3,16,4,512]{3,1,0,2:T(8,128)} %copy.1930), calls=%async_computation.1 | async-start | bytes 786432 | tf_op jit(solution)/shard_map/all_to_all | solution.py:138
  50.6 10.4 %copy-start.38 = (f32[3,16,4,512]{3,1,0,2:T(8,128)}, f32[3,16,4,512]{3,1,0,2:T(8,128)S(1)}, u32[]{:S(2)}) copy-start(f32[3,16,4,512]{3,1,0,2:T(8,128)S(1)} %all-to-all-done.1) | copy-start | bytes 1179652
  50.6 31.4 %all-to-all-start.2 = ((f32[9,16,4,512]{3,1,0,2:T(8,128)}), f32[9,16,4,512]{3,1,0,2:T(8,128)S(1)}, u32[]{:S(2)}, u32[]{:S(2)}) async-start(f32[9,16,4,512]{3,1,0,2:T(8,128)} %copy.1933), calls=%async_computation.2 | async-start | bytes 2359296 | tf_op jit(solution)/shard_map/all_to_all | solution.py:137
  462.0 8.1 %copy-start.1 = (f32[9,128,512]{1,2,0:T(8,128)S(1)}, f32[9,128,512]{1,2,0:T(8,128)}, u32[]{:S(2)}) copy-start(f32[9,128,512]{1,2,0:T(8,128)} %copy-done) | copy-start | bytes 7077892
  463.7 32.4 %all-to-all-start.3 = ((f32[9,16,4,512]{3,1,0,2:T(8,128)}), f32[9,16,4,512]{3,1,0,2:T(8,128)}, u32[]{:S(2)}, u32[]{:S(2)}) async-start(f32[9,16,4,512]{3,1,0,2:T(8,128)} %copy.1941), calls=%async_computation.3 | async-start | bytes 2359296 | tf_op jit(solution)/shard_map/all_to_all | solution.py:150
  526.2 9.3 %copy-start.30 = (f32[9,128,8,8,1]{1,4,3,2,0:T(1,128)S(1)}, f32[9,128,8,8,1]{1,4,3,2,0:T(1,128)}, u32[]{:S(2)}) copy-start(f32[9,128,8,8,1]{1,4,3,2,0:T(1,128)} %get-tuple-element.357) | copy-start | bytes 884740
  547.8 8.2 %copy-start.66 = (pred[128]{0:T(512)(128)(4,1)S(1)}, pred[128]{0:T(512)(128)(4,1)}, u32[]{:S(2)}) copy-start(pred[128]{0:T(512)(128)(4,1)} %get-tuple-element.432) | copy-start | bytes 388
  561.9 11.2 %copy-start.61 = (f32[128,64]{0,1:T(8,128)S(1)}, f32[128,64]{0,1:T(8,128)}, u32[]{:S(2)}) copy-start(f32[128,64]{0,1:T(8,128)} %get-tuple-element.426) | copy-start | bytes 98308
  561.9 13.4 %copy-start.60 = (f32[128,64]{0,1:T(8,128)S(1)}, f32[128,64]{0,1:T(8,128)}, u32[]{:S(2)}) copy-start(f32[128,64]{0,1:T(8,128)} %get-tuple-element.427) | copy-start | bytes 98308
  578.0 14.5 %copy-start.41 = (f32[9,128,1,8,8]{1,4,3,2,0:T(8,128)S(1)}, f32[9,128,1,8,8]{1,4,3,2,0:T(8,128)}, u32[]{:S(2)}) copy-start(f32[9,128,1,8,8]{1,4,3,2,0:T(8,128)} %get-tuple-element.364) | copy-start | bytes 884740
  595.7 9.2 %copy-start.59 = (f32[1,8192]{1,0:T(1,128)S(1)}, f32[1,8192]{1,0:T(1,128)}, u32[]{:S(2)}) copy-start(f32[1,8192]{1,0:T(1,128)} %concatenate.41) | copy-start | bytes 98308
  595.7 12.2 %copy-start.40 = (f32[9,128,1,8,8]{1,4,3,2,0:T(8,128)S(1)}, f32[9,128,1,8,8]{1,4,3,2,0:T(8,128)}, u32[]{:S(2)}) copy-start(f32[9,128,1,8,8]{1,4,3,2,0:T(8,128)} %get-tuple-element.365) | copy-start | bytes 884740
  606.8 29.4 %collective-permute-start.1 = (f32[10,8192]{1,0:T(8,128)}, f32[10,8192]{1,0:T(8,128)}, u32[]{:S(2)}, u32[]{:S(2)}) collective-permute-start(f32[10,8192]{1,0:T(8,128)} %pad_maximum_fusion.2), channel_id=1, source_target_pairs={{0,28},{4,0},{8,4},{12,8},{16,12},{20,16},{24,20},{28,24},{1,29},{... | collective-permute-start | bytes 983048 | tf_op jit(solution)/shard_map/ppermute | solution.py:26
  611.3 9.2 %copy-start.34 = (f32[9,128,64]{1,2,0:T(8,128)S(1)}, f32[9,128,64]{1,2,0:T(8,128)}, u32[]{:S(2)}) copy-start(f32[9,128,64]{1,2,0:T(8,128)} %copy-done.33) | copy-start | bytes 884740
  611.3 9.2 %copy-start.57 = (f32[128,64]{0,1:T(8,128)S(1)}, f32[128,64]{0,1:T(8,128)}, u32[]{:S(2)}) copy-start(f32[128,64]{0,1:T(8,128)} %copy.1988) | copy-start | bytes 98308
  620.6 8.4 %copy-start.46 = (f32[1,128,512]{1,2,0:T(8,128)S(1)}, f32[1,128,512]{1,2,0:T(8,128)}, u32[]{:S(2)}) copy-start(f32[1,128,512]{1,2,0:T(8,128)} %get-tuple-element.412) | copy-start | bytes 786436
  620.6 9.1 %copy-start.45 = (f32[1,128,512]{1,2,0:T(8,128)S(1)}, f32[1,128,512]{1,2,0:T(8,128)}, u32[]{:S(2)}) copy-start(f32[1,128,512]{1,2,0:T(8,128)} %get-tuple-element.411) | copy-start | bytes 786436
  620.6 9.8 %copy-start.35 = (f32[9,8192]{1,0:T(8,128)S(1)}, f32[9,8192]{1,0:T(8,128)}, u32[]{:S(2)}) copy-start(f32[9,8192]{1,0:T(8,128)} %concatenate.37) | copy-start | bytes 884740
  620.6 9.8 %copy-start.58 = (f32[1,8192]{1,0:T(1,128)S(1)}, f32[1,8192]{1,0:T(1,128)}, u32[]{:S(2)}) copy-start(f32[1,8192]{1,0:T(1,128)} %concatenate.38) | copy-start | bytes 98308
  622.4 8.8 %copy-start.44 = (f32[1,128,512]{1,2,0:T(8,128)S(1)}, f32[1,128,512]{1,2,0:T(8,128)}, u32[]{:S(2)}) copy-start(f32[1,128,512]{1,2,0:T(8,128)} %get-tuple-element.410) | copy-start | bytes 786436
  635.4 9.7 %collective-permute-start = (f32[10,8192]{1,0:T(8,128)}, f32[10,8192]{1,0:T(8,128)S(1)}, u32[]{:S(2)}, u32[]{:S(2)}) collective-permute-start(f32[10,8192]{1,0:T(8,128)} %pad_maximum_fusion.1), channel_id=1, source_target_pairs={{0,4},{4,8},{8,12},{12,16},{16,20},{20,24},{24,28},{28,0},{1,5},{5... | collective-permute-start | bytes 983048 | tf_op jit(solution)/shard_map/ppermute | solution.py:26
  (93 other events, 245.9 us)
where the time goes:
time: 686 us; the launch traced here: 673 us
  local copies, waits for them, and re-layouts  319 us (47%)
  matrix products  168 us (24%)
  other arithmetic  107 us (16%)
  waiting for transfers between devices  45.4 us (7%)
  starting transfers between devices  20.9 us (3%)
  loops' own time  9.53 us (1%)
    dot_general x60, matrix products, derive_all(): jnp.einsum(pattern, slope_table, volume, precision=highest)  168 us
    add x19, other arithmetic, elastic(): normal_y = lame_first * diverge + 2.0 * shear_modulus * slope_y[1]  33 us
    dot_general x21, local copies, waits for them, and re-layouts, derive_all(): jnp.einsum(pattern, slope_table, volume, precision=highest)  31.7 us
    gather x12, local copies, waits for them, and re-layouts, on_device(): jnp.take(chosen_values, target, axis=1)  27.2 us
    while x399, local copies, waits for them, and re-layouts  25.9 us
    add x20, other arithmetic, elastic(): speed_z = (slope_x[5] + slope_y[5] + slope_z[5]) / density  23.8 us
    all_to_all x1, waiting for transfers between devices, offload(): lax.all_to_all(unpacked.reshape(9, per_helper, helpers, node_total), 'hel...  22.7 us
    concatenate x4, local copies, waits for them, and re-layouts, rim_pack(): jnp.concatenate([face_values, face_speeds[None]], axis=0).reshape(10, -1)  22.3 us
  transfers between devices with their start and end apart: 6, of which 4 were waited for; matrix products, arithmetic and copies ran while one was open for 12% of the time, Pallas kernels for 0%

commit v1 on v0

v1 whole, which is shorter than its diff:
```python
import math

import jax
import jax.numpy as jnp
import ml_dtypes
import numpy as np
from jax import lax
from jax.experimental import pallas as pl
from jax.experimental.pallas import tpu as pltpu
from jax.sharding import PartitionSpec as P

P_SIZE = 8
ORD = 8
REF_MAX = 64
LANES = 128
TILES = 4
HALF = 64
SUB = 8

along_x = (6, 7, 8, 0, 3, 5)
along_y = (6, 7, 8, 3, 1, 4)
along_z = (6, 7, 8, 5, 4, 2)
both_yz = (6, 7, 8, 4)
pairs_yz = ((1, 2), (3, 5))
time_step = 0.5
VMEM_LIMIT = 56 * 1024 * 1024


def cheb_table(node_count):
    intervals = node_count - 1
    places = np.arange(node_count)
    points = np.cos(np.pi * places / intervals)
    weights = np.where((places == 0) | (places == intervals), 2.0, 1.0)
    scaled = weights * (-1.0) ** places
    differ = points[:, None] - points[None, :] + np.eye(node_count)
    matrix = np.outer(scaled, 1.0 / scaled) / differ
    matrix = matrix - np.eye(node_count) * np.sum(matrix, axis=1)[:, None]
    return matrix / (node_count * node_count / 4.0)


def taylor_weight(degree):
    return time_step ** (degree + 1) / math.factorial(degree + 1)


def tables():
    slope = cheb_table(P_SIZE).astype(np.float32).astype(np.float64)
    high = slope.astype(ml_dtypes.bfloat16).astype(np.float64)
    low = slope - high
    one = np.eye(P_SIZE)
    two = np.eye(2)

    def spread(matrix):
        along_b = np.kron(two, np.kron(matrix.T, one))
        along_e = np.kron(two, np.kron(one, matrix.T))
        return along_b, along_e

    hy, hz = spread(high)
    ly, lz = spread(low)
    none = np.zeros_like(hy)
    w1 = np.concatenate(
        [np.concatenate([hy, hz], 1), np.concatenate([hy, hz], 1), np.concatenate([ly, lz], 1)], 0
    )
    diag_high = np.block([[hy, none], [none, hz]])
    diag_low = np.block([[ly, none], [none, lz]])
    w2 = np.concatenate([diag_high, diag_high, diag_low], 0)

    half = P_SIZE // 2
    top = slope[:half, :half]
    mirror = slope[:half, ::-1][:, :half]
    parts = ((top + mirror) / 2, (top - mirror) / 2)
    lane_half = np.arange(LANES) // HALF
    rows = []
    for part in parts:
        for t in range(2):
            for s in range(2):
                for swap in range(2):
                    source = lane_half if swap == 0 else 1 - lane_half
                    rows.append(part[2 * t + lane_half, 2 * s + source])
    xc = np.broadcast_to(np.stack(rows)[:, None, :], (len(rows), SUB, LANES))
    return (
        jnp.asarray(w1.astype(ml_dtypes.bfloat16)),
        jnp.asarray(w2.astype(ml_dtypes.bfloat16)),
        jnp.asarray(np.ascontiguousarray(xc).astype(np.float32)),
    )


def roll(value, by):
    by = by % LANES
    return value if by == 0 else pltpu.roll(value, by, value.ndim - 1)


def lane_ids(rows):
    return lax.broadcasted_iota(jnp.int32, (rows, LANES), 1)


def split(value):
    high = value.astype(jnp.bfloat16)
    return high, (value - high.astype(jnp.float32)).astype(jnp.bfloat16)


def x_slope(parts, xc_ref):
    mirrored = [roll(parts[3 - t], HALF) for t in range(2)]
    even = [parts[t] + mirrored[t] for t in range(2)]
    odd = [parts[t] - mirrored[t] for t in range(2)]
    sources = [[even, [roll(v, HALF) for v in even]], [odd, [roll(v, HALF) for v in odd]]]
    result = [None] * TILES
    for t in range(2):
        sums = []
        for kind in range(2):
            total = None
            for s in range(2):
                for swap in range(2):
                    term = sources[kind][swap][s] * xc_ref[((kind * 2 + t) * 2 + s) * 2 + swap]
                    total = term if total is None else total + term
            sums.append(total)
        result[t] = sums[0] + sums[1]
        result[3 - t] = roll(sums[1] - sums[0], HALF)
    return result


def apply_operator(load, material, tabs, scratch, rows, scale, emit):
    w1_ref, w2_ref, xc_ref = tabs
    a1, a2, o1, o2 = scratch
    for i, f in enumerate(both_yz):
        for t in range(TILES):
            high, low = split(load(f, 0, rows, t))
            at = pl.ds((i * TILES + t) * rows, rows)
            a1[at, 0:LANES] = high
            a1[at, LANES : 2 * LANES] = low
            a1[at, 2 * LANES : 3 * LANES] = high
    for i, pair in enumerate(pairs_yz):
        for t in range(TILES):
            at = pl.ds((i * TILES + t) * rows, rows)
            for place, f in enumerate(pair):
                high, low = split(load(f, 0, rows, t))
                for block, piece in ((0, high), (2, low), (4, high)):
                    column = (block + place) * LANES
                    a2[at, column : column + LANES] = piece
    o1[...] = jnp.dot(a1[...], w1_ref[...], preferred_element_type=jnp.float32)
    o2[...] = jnp.dot(a2[...], w2_ref[...], preferred_element_type=jnp.float32)

    def yz(ref, i, t, r):
        at = pl.ds((i * TILES + t) * rows + r, SUB)
        return ref[at, 0:LANES], ref[at, LANES : 2 * LANES]

    for r in range(0, rows, SUB):
        slopes = {f: x_slope([load(f, r, SUB, t) for t in range(TILES)], xc_ref) for f in along_x}
        factor = scale(r)
        for t in range(TILES):
            lame, shear, light = [
                m if factor is None else m * factor for m in material(r, t)
            ]
            shear_2 = shear + shear
            dy_vx, dz_vx = yz(o1, 0, t, r)
            dy_vy, dz_vy = yz(o1, 1, t, r)
            dy_vz, dz_vz = yz(o1, 2, t, r)
            dy_syz, dz_syz = yz(o1, 3, t, r)
            dy_syy, dz_szz = yz(o2, 0, t, r)
            dy_sxy, dz_sxz = yz(o2, 1, t, r)
            dx_vx, dx_vy, dx_vz = (slopes[f][t] for f in (6, 7, 8))
            diverge = lame * (dx_vx + dy_vy + dz_vz)
            emit(0, r, t, diverge + shear_2 * dx_vx)
            emit(1, r, t, diverge + shear_2 * dy_vy)
            emit(2, r, t, diverge + shear_2 * dz_vz)
            emit(3, r, t, shear * (dy_vx + dx_vy))
            emit(4, r, t, shear * (dz_vy + dy_vz))
            emit(5, r, t, shear * (dz_vx + dx_vz))
            emit(6, r, t, light * (slopes[0][t] + dy_sxy + dz_sxz))
            emit(7, r, t, light * (slopes[3][t] + dy_syy + dz_syz))
            emit(8, r, t, light * (slopes[5][t] + dy_syz + dz_szz))


def span(tile):
    return slice(tile * LANES, (tile + 1) * LANES)


def pack_faces(read, rows):
    low = lane_ids(rows // 2) < HALF
    first, second = read(0, 0), read(rows // 2, 0)
    start = jnp.where(low, first, roll(second, HALF))
    first, second = read(0, 3), read(rows // 2, 3)
    end = jnp.where(low, roll(first, HALF), second)
    return end, start


def wave_speed(density, lame, shear):
    return jnp.sqrt((lame + 2.0 * shear) / density)


def early_kernel(sol_ref, mat_ref, edge_ref, w1_ref, w2_ref, xc_ref, out_ref, end_ref, start_ref, a1, a2, o1, o2):
    rows = sol_ref.shape[1]
    load = lambda f, r, count, t: sol_ref[f, r : r + count, span(t)]
    material = lambda r, t: (
        mat_ref[1, r : r + SUB, span(t)],
        mat_ref[2, r : r + SUB, span(t)],
        1.0 / mat_ref[0, r : r + SUB, span(t)],
    )

    def emit(f, r, t, value):
        base = time_step * sol_ref[f, r : r + SUB, span(t)]
        out_ref[f, r : r + SUB, span(t)] = base + value

    apply_operator(
        load, material, (w1_ref, w2_ref, xc_ref), (a1, a2, o1, o2), rows, lambda r: taylor_weight(1), emit
    )
    count = rows // 2
    for f in range(9):
        end, start = pack_faces(lambda r, t, f=f: out_ref[f, r : r + count, span(t)], rows)
        end_ref[f] = end
        start_ref[f] = start
    for i, ref in enumerate((edge_ref, mat_ref)):

        def speed(r, t, ref=ref):
            return wave_speed(*[ref[m, r : r + count, span(t)] for m in range(3)])

        end, start = pack_faces(speed, rows)
        end_ref[9 + i] = end
        start_ref[9 + i] = start


def refined_kernel(count_ref, sol_ref, mat_ref, w1_ref, w2_ref, xc_ref, out_ref, end_ref, start_ref, state, light, a1, a2, o1, o2):
    rows = sol_ref.shape[1]
    limit = count_ref[0, 0]
    for f in range(9):
        first = time_step * sol_ref[f]
        state[f] = first
        out_ref[f] = first
    light[...] = 1.0 / mat_ref[0]
    load = lambda f, r, count, t: state[f, r : r + count, span(t)]
    material = lambda r, t: (
        mat_ref[1, r : r + SUB, span(t)],
        mat_ref[2, r : r + SUB, span(t)],
        light[r : r + SUB, span(t)],
    )

    def emit(f, r, t, value):
        state[f, r : r + SUB, span(t)] = value
        out_ref[f, r : r + SUB, span(t)] = out_ref[f, r : r + SUB, span(t)] + value

    def term(degree, carry):
        ratio = time_step / jnp.full((SUB, LANES), degree + 1, jnp.int32).astype(jnp.float32)
        bound = jnp.where(degree < 2, rows, limit)

        def scale(r):
            ids = r + lax.broadcasted_iota(jnp.int32, (SUB, LANES), 0)
            return jnp.where(ids < bound, ratio, 0.0)

        apply_operator(load, material, (w1_ref, w2_ref, xc_ref), (a1, a2, o1, o2), rows, scale, emit)
        return carry

    lax.fori_loop(1, ORD, term, 0)
    count = rows // 2
    for f in range(9):
        end, start = pack_faces(lambda r, t, f=f: out_ref[f, r : r + count, span(t)], rows)
        end_ref[f] = end
        start_ref[f] = start


def hot(row, first, count):
    cells = row.shape[1]
    ids = first + lax.broadcasted_iota(jnp.int32, (count, cells), 0)
    return jnp.where(ids == row, 1.0, 0.0).T


def unpack_faces(after, before):
    low = lane_ids(after.shape[0]) < HALF
    return jnp.concatenate(
        [
            jnp.where(low, after, 0.0),
            jnp.where(low, roll(after, HALF), 0.0),
            jnp.where(low, 0.0, roll(before, HALF)),
            jnp.where(low, 0.0, before),
        ],
        0,
    )


def flux(direction, jump, far_less, lame, shear, light, speed, sign):
    members = ((6, 7, 8, 0, 3, 5), (6, 7, 8, 3, 1, 4), (6, 7, 8, 5, 4, 2))[direction]
    g = [jump[m] for m in members]
    through = g[direction]
    spread_out = lame * through
    normal = [spread_out, spread_out, spread_out, None, None, None, light * g[3], light * g[4], light * g[5]]
    normal[direction] = spread_out + 2.0 * (shear * through)
    if direction == 0:
        normal[3], normal[5] = shear * g[1], shear * g[2]
    elif direction == 1:
        normal[3], normal[4] = shear * g[0], shear * g[2]
    else:
        normal[4], normal[5] = shear * g[1], shear * g[0]
    return [
        speed * jump[f] if normal[f] is None else normal[f] + speed * jump[f] for f in range(9)
    ]


def correct_kernel(
    sol_ref, mat_ref, low_ref, high_ref, near_ref, after_ref, before_ref, w1_ref, w2_ref, xc_ref,
    out_ref, xmat_ref, late_ref, a1, a2, o1, o2, compact, hot_ref, rhs, far, fix, light,
):
    cells = sol_ref.shape[1]
    half = low_ref.shape[1]
    lanes = lane_ids(SUB)
    light[...] = 1.0 / mat_ref[0]

    def integral(f, r, count, t):
        if r < half:
            return low_ref[f, r : r + count, span(t)]
        return high_ref[f, r - half : r - half + count, span(t)]

    step = (0, 16, 2)
    shift = (0, 56, 7)
    in_y = (lanes % HALF < 8) | (lanes % HALF >= 56)
    in_z = (lanes % 8 == 0) | (lanes % 8 == 7)
    starts = (lanes < HALF, lanes % HALF < 0, lanes % 8 < 0)

    def squeeze(read, direction):
        if direction == 0:
            return jnp.where(lanes < HALF, read(0), read(3))
        inside = (None, in_y, in_z)[direction]
        total = read(0)
        for t in range(1, TILES):
            mask = owner[direction] == t
            total = jnp.where(mask, roll(read(t), step[direction] * t), total)
        return total

    owner = (None, ((lanes + 72) % HALF) // 16, ((lanes + 1) % 8) // 2)
    y_home = (lanes - 16 * owner[1] + LANES) % LANES
    z_home = (lanes - 2 * owner[2] + LANES) % LANES
    first = (lanes < HALF, y_home % HALF < 8, z_home % 8 == 0)

    for direction in range(3):
        for r in range(0, cells, SUB):
            at = pl.ds(r, SUB)
            for f in range(9):
                compact[direction, f, at, :] = squeeze(lambda t: integral(f, r, SUB, t), direction)
            density = squeeze(lambda t: mat_ref[0, at, span(t)], direction)
            lame = squeeze(lambda t: mat_ref[1, at, span(t)], direction)
            shear = squeeze(lambda t: mat_ref[2, at, span(t)], direction)
            side = jnp.where(first[direction], 0.25, -0.25)
            compact[direction, 9, at, :] = wave_speed(density, lame, shear)
            compact[direction, 10, at, :] = side * lame
            compact[direction, 11, at, :] = side * shear
            compact[direction, 12, at, :] = side / density

    here = near_ref[...] % cells
    for direction in (1, 2):
        plus = hot(here[2 * direction + 1 : 2 * direction + 2], 0, cells).astype(jnp.bfloat16)
        minus = hot(here[2 * direction : 2 * direction + 1], 0, cells).astype(jnp.bfloat16)
        for k in range(2):
            hot_ref[:, 2 * k * LANES : (2 * k + 1) * LANES] = plus
            hot_ref[:, (2 * k + 1) * LANES : (2 * k + 2) * LANES] = minus
        starting = jnp.broadcast_to(first[direction][0:1], (cells, LANES))
        for f in range(10):
            own = compact[direction, f]
            up = jnp.where(starting, roll(own, -shift[direction]), 0.0)
            down = jnp.where(starting, 0.0, roll(own, shift[direction]))
            for k, piece in enumerate((up, down)):
                high, low = split(piece)
                rhs[k * LANES : (k + 1) * LANES, span(f)] = high
                rhs[(k + 2) * LANES : (k + 3) * LANES, span(f)] = low
        far[...] = jnp.dot(hot_ref[...], rhs[...], preferred_element_type=jnp.float32)
        for r in range(0, cells, SUB):
            at = pl.ds(r, SUB)
            jump = [far[at, span(f)] - compact[direction, f, at, :] for f in range(9)]
            speed = 0.25 * jnp.maximum(far[at, span(9)], compact[direction, 9, at, :])
            lame, shear, weight = (compact[direction, i, at, :] for i in (10, 11, 12))
            for f, value in enumerate(flux(direction, jump, None, lame, shear, weight, speed, None)):
                fix[direction, f, at, :] = value

    plus = here[1:2]
    minus = here[0:1]
    pieces = [hot(plus, half, half), hot(minus, half, half), hot(plus, 0, half), hot(minus, 0, half)]
    early = jnp.concatenate(pieces[:2], 1).astype(jnp.bfloat16)
    late = jnp.concatenate(pieces[2:], 1).astype(jnp.bfloat16)
    late_ref[:, :LANES] = late
    late_ref[:, LANES:] = late
    hot_ref[:, 0 * LANES : 1 * LANES] = early
    hot_ref[:, 1 * LANES : 2 * LANES] = early
    hot_ref[:, 2 * LANES : 3 * LANES] = late
    hot_ref[:, 3 * LANES : 4 * LANES] = late
    for f in range(9):
        high, low = split(unpack_faces(after_ref[f], before_ref[f]))
        rhs[0:LANES, span(f)] = high
        rhs[LANES : 2 * LANES, span(f)] = low
    for k, f in ((0, 10), (2, 9)):
        high, low = split(unpack_faces(after_ref[f], before_ref[f]))
        rhs[k * LANES : (k + 1) * LANES, span(9)] = high
        rhs[(k + 1) * LANES : (k + 2) * LANES, span(9)] = low
    far[:, : 9 * LANES] = jnp.dot(
        hot_ref[:, : 2 * LANES], rhs[: 2 * LANES, : 9 * LANES], preferred_element_type=jnp.float32
    )
    far[:, span(9)] = jnp.dot(hot_ref[...], rhs[:, span(9)], preferred_element_type=jnp.float32)
    for r in range(0, cells, SUB):
        at = pl.ds(r, SUB)
        jump = [far[at, span(f)] - compact[0, f, at, :] for f in range(9)]
        speed = 0.25 * jnp.maximum(far[at, span(9)], compact[0, 9, at, :])
        lame, shear, weight = (compact[0, i, at, :] for i in (10, 11, 12))
        for f, value in enumerate(flux(0, jump, None, lame, shear, weight, speed, None)):
            fix[0, f, at, :] = value
        for i, value in enumerate((lame, shear, weight, speed)):
            xmat_ref[i, at, :] = value

    for start in range(0, cells, half):
        load = lambda f, r, count, t: integral(f, start + r, count, t)
        material = lambda r, t: (
            mat_ref[1, start + r : start + r + SUB, span(t)],
            mat_ref[2, start + r : start + r + SUB, span(t)],
            light[start + r : start + r + SUB, span(t)],
        )

        def emit(f, r, t, value):
            at = pl.ds(start + r, SUB)
            total = sol_ref[f, at, span(t)] + value
            total = total + jnp.where(in_y, roll(fix[1, f, at, :], -step[1] * t), 0.0)
            total = total + jnp.where(in_z, roll(fix[2, f, at, :], -step[2] * t), 0.0)
            if t == 0:
                total = total + jnp.where(lanes < HALF, fix[0, f, at, :], 0.0)
            if t == TILES - 1:
                total = total + jnp.where(lanes < HALF, 0.0, fix[0, f, at, :])
            out_ref[f, at, span(t)] = total

        apply_operator(
            load, material, (w1_ref, w2_ref, xc_ref), (a1, a2, o1, o2), half, lambda r: None, emit
        )


def finish_kernel(done_ref, after_ref, before_ref, xmat_ref, late_ref, out_ref, ends, rhs, far, sems):
    cells = ends.shape[2]
    places = (0, TILES - 1)
    loads = [
        pltpu.make_async_copy(done_ref.at[:, :, pl.ds(t * LANES, LANES)], ends.at[i], sems.at[i])
        for i, t in enumerate(places)
    ]
    for copy in loads:
        copy.start()
    for f in range(9):
        high, low = split(unpack_faces(after_ref[f], before_ref[f]))
        rhs[0:LANES, span(f)] = high
        rhs[LANES : 2 * LANES, span(f)] = low
    far[...] = jnp.dot(late_ref[...], rhs[...], preferred_element_type=jnp.float32)
    for copy in loads:
        copy.wait()
    low_half = lane_ids(SUB) < HALF
    for r in range(0, cells, SUB):
        at = pl.ds(r, SUB)
        jump = [far[at, span(f)] for f in range(9)]
        lame, shear, weight, speed = (xmat_ref[i, at, :] for i in range(4))
        for f, value in enumerate(flux(0, jump, None, lame, shear, weight, speed, None)):
            ends[0, f, at, :] = ends[0, f, at, :] + jnp.where(low_half, value, 0.0)
            ends[1, f, at, :] = ends[1, f, at, :] + jnp.where(low_half, 0.0, value)
    stores = [
        pltpu.make_async_copy(ends.at[i], out_ref.at[:, :, pl.ds(t * LANES, LANES)], sems.at[i])
        for i, t in enumerate(places)
    ]
    for copy in stores:
        copy.start()
    for copy in stores:
        copy.wait()


def shifted(value, axis, by):
    peers = lax.axis_size(axis)
    return lax.ppermute(value, axis, [(i, (i + by) % peers) for i in range(peers)])


def block(shape, *place):
    return pl.BlockSpec(shape, lambda i: place)


def whole(shape):
    return pl.BlockSpec(shape, lambda i: (0,) * len(shape))


def f32(*shape):
    return jax.ShapeDtypeStruct(shape, jnp.float32)


def operator_scratch(rows):
    return [
        pltpu.VMEM((len(both_yz) * TILES * rows, 3 * LANES), jnp.bfloat16),
        pltpu.VMEM((len(pairs_yz) * TILES * rows, 6 * LANES), jnp.bfloat16),
        pltpu.VMEM((len(both_yz) * TILES * rows, 2 * LANES), jnp.float32),
        pltpu.VMEM((len(pairs_yz) * TILES * rows, 2 * LANES), jnp.float32),
    ]


def on_device(solution, material, neighbours, refine_count):
    cells, nodes = solution.shape[1:]
    rows = REF_MAX
    w1, w2, xc = tables()
    params = pltpu.CompilerParams(vmem_limit_bytes=VMEM_LIMIT)
    table_specs = [whole(w1.shape), whole(w2.shape), whole(xc.shape)]
    early_shape, late_shape = (11, rows // 2, LANES), (9, rows // 2, LANES)

    high, end, start = pl.pallas_call(
        early_kernel,
        grid=(1,),
        in_specs=[
            block((9, rows, nodes), 0, 1, 0),
            block((3, rows, nodes), 0, 1, 0),
            block((3, rows, nodes), 0, 0, 0),
        ]
        + table_specs,
        out_specs=[whole((9, rows, nodes)), whole(early_shape), whole(early_shape)],
        out_shape=[f32(9, rows, nodes), f32(*early_shape), f32(*early_shape)],
        scratch_shapes=operator_scratch(rows),
        compiler_params=params,
        name="early",
    )(solution, material, material, w1, w2, xc)
    early_after = shifted(end, "space", -1)
    early_before = shifted(start, "space", 1)

    low, end, start = pl.pallas_call(
        refined_kernel,
        grid=(1,),
        in_specs=[
            pl.BlockSpec(memory_space=pltpu.SMEM),
            block((9, rows, nodes), 0, 0, 0),
            block((3, rows, nodes), 0, 0, 0),
        ]
        + table_specs,
        out_specs=[whole((9, rows, nodes)), whole(late_shape), whole(late_shape)],
        out_shape=[f32(9, rows, nodes), f32(*late_shape), f32(*late_shape)],
        scratch_shapes=[
            pltpu.VMEM((9, rows, nodes), jnp.float32),
            pltpu.VMEM((rows, nodes), jnp.float32),
        ]
        + operator_scratch(rows),
        compiler_params=params,
        name="refined",
    )(refine_count, solution, material, w1, w2, xc)
    late_after = shifted(end, "space", -1)
    late_before = shifted(start, "space", 1)

    done, xmat, late_hot = pl.pallas_call(
        correct_kernel,
        grid=(1,),
        in_specs=[
            whole(solution.shape),
            whole(material.shape),
            whole(low.shape),
            whole(high.shape),
            whole(neighbours.shape),
            whole(early_shape),
            whole(early_shape),
        ]
        + table_specs,
        out_specs=[whole(solution.shape), whole((4, cells, LANES)), whole((cells, 2 * LANES))],
        out_shape=[
            f32(*solution.shape),
            f32(4, cells, LANES),
            jax.ShapeDtypeStruct((cells, 2 * LANES), jnp.bfloat16),
        ],
        scratch_shapes=operator_scratch(rows)
        + [
            pltpu.VMEM((3, 13, cells, LANES), jnp.float32),
            pltpu.VMEM((cells, 4 * LANES), jnp.bfloat16),
            pltpu.VMEM((4 * LANES, 10 * LANES), jnp.bfloat16),
            pltpu.VMEM((cells, 10 * LANES), jnp.float32),
            pltpu.VMEM((3, 9, cells, LANES), jnp.float32),
            pltpu.VMEM((cells, nodes), jnp.float32),
        ],
        compiler_params=params,
        name="correct",
    )(solution, material, low, high, neighbours, early_after, early_before, w1, w2, xc)

    return pl.pallas_call(
        finish_kernel,
        grid=(1,),
        in_specs=[
            pl.BlockSpec(memory_space=pl.ANY),
            whole(late_shape),
            whole(late_shape),
            whole(xmat.shape),
            whole(late_hot.shape),
        ],
        out_specs=pl.BlockSpec(memory_space=pl.ANY),
        out_shape=f32(*solution.shape),
        scratch_shapes=[
            pltpu.VMEM((2, 9, cells, LANES), jnp.float32),
            pltpu.VMEM((2 * LANES, 9 * LANES), jnp.bfloat16),
            pltpu.VMEM((cells, 9 * LANES), jnp.float32),
            pltpu.SemaphoreType.DMA((2,)),
        ],
        input_output_aliases={0: 0},
        compiler_params=params,
        name="finish",
    )(done, late_after, late_before, xmat, late_hot)


def solution(mesh):
    in_specs = (
        P(None, ("space", "help"), None),
        P(None, ("space", "help"), None),
        P(None, ("space", "help")),
        P("space", "help"),
    )
    out_specs = P(None, ("space", "help"), None)
    return jax.shard_map(
        on_device, mesh=mesh, in_specs=in_specs, out_specs=out_specs, check_vma=False
    )
```

time: 686 us -> 69 us (0.10); the launches traced: 673 us -> 68.8 us
  local copies, waits for them, and re-layouts: 319 us -> 1.44 us
  matrix products: 168 us -> 0 us
  other arithmetic: 107 us -> 0 us
  Pallas kernels: 0 us -> 60.7 us
  waiting for transfers between devices: 45.4 us -> 0.01 us
  starting transfers between devices: 20.9 us -> 5.98 us
  loops' own time: 9.53 us -> 0 us
    dot_general x60 -> x0, matrix products: 168 us -> none  [derive_all(): jnp.einsum(pattern, slope_table, volume, precision=highest)]
    add x65 -> x0, other arithmetic: 70.7 us -> none  [the longest x19 33 us: elastic(): normal_y = lame_first * diverge + 2.0 * shear_modulus * slope_y[1]]
    add x174 -> x0, local copies, waits for them, and re-layouts: 65.6 us -> none  [the longest x18 19.8 us: elastic(): normal_x = lame_first * diverge + 2.0 * shear_modulus * slope_x[0]]
    pallas_call x0 -> x4, Pallas kernels: none -> 60.7 us  [the longest x1 27.8 us: on_device(): pl.pallas_call(refined_kernel, grid=(1,), in_specs=[pl.BlockSpec(memory_s...]
    all_to_all x4 -> x0, waiting for transfers between devices: 41.9 us -> none  [the longest x1 22.7 us: offload(): lax.all_to_all(unpacked.reshape(9, per_helper, helpers, node_total), 'hel...]
    gather x21 -> x0, local copies, waits for them, and re-layouts: 37.5 us -> none  [the longest x12 27.2 us: on_device(): jnp.take(chosen_values, target, axis=1)]
    dot_general x21 -> x0, local copies, waits for them, and re-layouts: 31.7 us -> none  [derive_all(): jnp.einsum(pattern, slope_table, volume, precision=highest)]
    slice x79 -> x0, local copies, waits for them, and re-layouts: 29.3 us -> none  [the longest x7 13 us: face_trace(): lax.index_in_dim(volume, place, axis=len(shape) + direction, keepdims=False)]
  transfers between devices with their start and end apart: 6 -> 4, of which waited for: 4 -> 0; matrix products, arithmetic and copies ran while one was open for 12% -> 0% of each run, Pallas kernels for 0% -> 72%
where the time goes in v1:
time: 69 us; the launch traced here: 68.8 us
  Pallas kernels  60.7 us (88%)
  starting transfers between devices  5.98 us (9%)
  local copies, waits for them, and re-layouts  1.44 us (2%)
  between operations  0.7 us (1%)
    pallas_call x1, Pallas kernels, on_device(): pl.pallas_call(refined_kernel, grid=(1,), in_specs=[pl.BlockSpec(memory_s...  27.8 us
    pallas_call x1, Pallas kernels, on_device(): pl.pallas_call(correct_kernel, grid=(1,), in_specs=[whole(solution.shape)...  21.5 us
    pallas_call x1, Pallas kernels, on_device(): pl.pallas_call(early_kernel, grid=(1,), in_specs=[block((9, rows, nodes),...  7.82 us
    ppermute x4, starting transfers between devices, shifted(): lax.ppermute(value, axis, [(i, (i + by) % peers) for i in range(peers)])  5.98 us
    pallas_call x1, Pallas kernels, on_device(): pl.pallas_call(finish_kernel, grid=(1,), in_specs=[pl.BlockSpec(memory_sp...  3.55 us
    unnamed x8, local copies, waits for them, and re-layouts  1.44 us
  transfers between devices with their start and end apart: 4, of which 0 were waited for; matrix products, arithmetic and copies ran while one was open for 0% of the time, Pallas kernels for 72%

profile of v1, /device:TPU:0, one launch (start us, length us, event | category | flops | bytes accessed | tf_op | source)
XLA Modules:
  0.0 68.8 jit_solution(14970691579567986216)
XLA Ops:
  0.0 7.8 %early.1 = (f32[9,64,512]{2,1,0:T(8,128)}, f32[11,32,128]{2,1,0:T(8,128)}, f32[11,32,128]{2,1,0:T(8,128)}) custom-call(f32[9,128,512]{2,1,0:T(8,128)} %sol_ref.5, f32[3,128,512]{2,1,0:T(8,128)} %mat_ref.5, f32[3,128,512]{2,1,0:T(8,128)} %mat_ref.5, bf16[384,256]{1,0:T(8,128)(2,1)} %constant.6.clone.w1_ref, bf16[768,256]{1,0:T(8,128)(2,1)} %constant.7.clone.w2_ref, ...), custom_call_target="tpu_custom_call" | custom-call | tf_op jit(solution)/shard_map/early/pallas_call | solution.py:495
  7.8 3.3 %collective-permute-start = (f32[11,32,128]{2,1,0:T(8,128)}, f32[11,32,128]{2,1,0:T(8,128)S(1)}, u32[]{:S(2)}, u32[]{:S(2)}) collective-permute-start(f32[11,32,128]{2,1,0:T(8,128)} %get-tuple-element.16), channel_id=1, source_target_pairs={{0,28},{4,0},{8,4},{12,8},{16,12},{20,16},{24,20},{28,24},{1,29},{... | collective-permute-start | bytes 540680 | tf_op jit(solution)/shard_map/ppermute | solution.py:463
  11.2 0.0 collective-permute-start.1
  11.8 27.8 %refined.1 = (f32[9,64,512]{2,1,0:T(8,128)}, f32[9,32,128]{2,1,0:T(8,128)}, f32[9,32,128]{2,1,0:T(8,128)}) custom-call(s32[1,1]{1,0:T(1,128)S(6)} %copy.10.count_ref, f32[9,128,512]{2,1,0:T(8,128)} %sol_ref.5, f32[3,128,512]{2,1,0:T(8,128)} %mat_ref.5, bf16[384,256]{1,0:T(8,128)(2,1)} %constant.6.clone.w1_ref, bf16[768,256]{1,0:T(8,128)(2,1)} %constant.7.clone.w2_ref, ...), custom_call_target="tpu_custom_call" | custom-call | tf_op jit(solution)/shard_map/refined/pallas_call | solution.py:513
  39.7 2.6 %collective-permute-start.2 = (f32[9,32,128]{2,1,0:T(8,128)}, f32[9,32,128]{2,1,0:T(8,128)S(1)}, u32[]{:S(2)}, u32[]{:S(2)}) collective-permute-start(f32[9,32,128]{2,1,0:T(8,128)} %get-tuple-element.19), channel_id=1, source_target_pairs={{0,28},{4,0},{8,4},{12,8},{16,12},{20,16},{24,20},{28,24},{1,29},{... | collective-permute-start | bytes 442376 | tf_op jit(solution)/shard_map/ppermute | solution.py:463
  42.3 0.0 collective-permute-start.3
  42.3 0.0 collective-permute-done.after_ref
  42.3 0.0 copy-start
  42.3 0.0 collective-permute-done.1.before_ref
  42.3 0.0 copy-start.1
  42.3 0.6 copy-done
  43.0 0.1 copy-done.1
  43.1 21.5 %correct.1 = (f32[9,128,512]{2,1,0:T(8,128)}, f32[4,128,128]{2,1,0:T(8,128)}, bf16[128,256]{1,0:T(8,128)(2,1)}) custom-call(f32[9,128,512]{2,1,0:T(8,128)} %sol_ref.5, f32[3,128,512]{2,1,0:T(8,128)} %mat_ref.5, f32[9,64,512]{2,1,0:T(8,128)} %get-tuple-element.14.low_ref, f32[9,64,512]{2,1,0:T(8,128)} %get-tuple-element.15.high_ref, s32[6,128]{1,0:T(8,128)} %near_ref.1, ...), custom_call_target="tpu_custom_call" | custom-call | tf_op jit(solution)/shard_map/correct/pallas_call | solution.py:535
  64.5 0.0 collective-permute-done.2.after_ref
  64.5 0.0 copy-start.2
  64.5 0.0 collective-permute-done.3.before_ref
  64.5 0.0 copy-start.3
  64.5 0.6 copy-done.2
  65.2 0.1 copy-done.3
  65.2 3.5 %finish.1 = f32[9,128,512]{2,1,0:T(8,128)} custom-call(f32[9,128,512]{2,1,0:T(8,128)} %get-tuple-element.18.done_ref, f32[9,32,128]{2,1,0:T(8,128)} %copy-done.2, f32[9,32,128]{2,1,0:T(8,128)} %copy-done.3, f32[4,128,128]{2,1,0:T(8,128)} %get-tuple-element.21.xmat_ref, bf16[128,256]{1,0:T(8,128)(2,1)} %get-tuple-element.22.late_ref), custom_call_target="tpu_custom_call", output_to_operand_aliasing={{}: (0, {})} | custom-call | tf_op jit(solution)/shard_map/finish/pallas_call | solution.py:567
Async XLA Ops:
  7.8 34.5 %collective-permute-start = (f32[11,32,128]{2,1,0:T(8,128)}, f32[11,32,128]{2,1,0:T(8,128)S(1)}, u32[]{:S(2)}, u32[]{:S(2)}) collective-permute-start(f32[11,32,128]{2,1,0:T(8,128)} %get-tuple-element.16), channel_id=1, source_target_pairs={{0,28},{4,0},{8,4},{12,8},{16,12},{20,16},{24,20},{28,24},{1,29},{... | collective-permute-start | bytes 540680 | tf_op jit(solution)/shard_map/ppermute | solution.py:463
  11.2 31.1 %collective-permute-start.1 = (f32[11,32,128]{2,1,0:T(8,128)}, f32[11,32,128]{2,1,0:T(8,128)S(1)}, u32[]{:S(2)}, u32[]{:S(2)}) collective-permute-start(f32[11,32,128]{2,1,0:T(8,128)} %get-tuple-element.17), channel_id=1, source_target_pairs={{0,4},{4,8},{8,12},{12,16},{16,20},{20,24},{24,28},{28,0},{1,5},{5... | collective-permute-start | bytes 540680 | tf_op jit(solution)/shard_map/ppermute | solution.py:463
  39.7 24.9 %collective-permute-start.2 = (f32[9,32,128]{2,1,0:T(8,128)}, f32[9,32,128]{2,1,0:T(8,128)S(1)}, u32[]{:S(2)}, u32[]{:S(2)}) collective-permute-start(f32[9,32,128]{2,1,0:T(8,128)} %get-tuple-element.19), channel_id=1, source_target_pairs={{0,28},{4,0},{8,4},{12,8},{16,12},{20,16},{24,20},{28,24},{1,29},{... | collective-permute-start | bytes 442376 | tf_op jit(solution)/shard_map/ppermute | solution.py:463
  42.3 22.2 %collective-permute-start.3 = (f32[9,32,128]{2,1,0:T(8,128)}, f32[9,32,128]{2,1,0:T(8,128)S(1)}, u32[]{:S(2)}, u32[]{:S(2)}) collective-permute-start(f32[9,32,128]{2,1,0:T(8,128)} %get-tuple-element.20), channel_id=1, source_target_pairs={{0,4},{4,8},{8,12},{12,16},{16,20},{20,24},{24,28},{28,0},{1,5},{5... | collective-permute-start | bytes 442376 | tf_op jit(solution)/shard_map/ppermute | solution.py:463
  42.3 0.7 copy-start
  42.3 0.7 %copy-start.1 = (f32[11,32,128]{2,1,0:T(8,128)}, f32[11,32,128]{2,1,0:T(8,128)S(1)}, u32[]{:S(2)}) copy-start(f32[11,32,128]{2,1,0:T(8,128)S(1)} %collective-permute-done.1.before_ref) | copy-start | bytes 540676
  64.5 0.7 copy-start.2
  64.5 0.7 %copy-start.3 = (f32[9,32,128]{2,1,0:T(8,128)}, f32[9,32,128]{2,1,0:T(8,128)S(1)}, u32[]{:S(2)}) copy-start(f32[9,32,128]{2,1,0:T(8,128)S(1)} %collective-permute-done.3.before_ref) | copy-start | bytes 442372

commit v2 on v1

v2 whole, which is shorter than its diff:
```python
import math

import jax
import jax.numpy as jnp
import ml_dtypes
import numpy as np
from jax import lax
from jax.experimental import pallas as pl
from jax.experimental.pallas import tpu as pltpu
from jax.sharding import PartitionSpec as P

P_SIZE = 8
ORD = 8
REF_MAX = 64
LANES = 128
TILES = 4
HALF = 64
SUB = 8
OPERATOR_SCRATCH = 6
LOADED = 7

along_x = (6, 7, 8, 0, 3, 5)
along_y = (6, 7, 8, 3, 1, 4)
along_z = (6, 7, 8, 5, 4, 2)
both_yz = (6, 7, 8, 4)
pairs_yz = ((1, 2), (3, 5))
time_step = 0.5


def cheb_table(node_count):
    intervals = node_count - 1
    places = np.arange(node_count)
    points = np.cos(np.pi * places / intervals)
    weights = np.where((places == 0) | (places == intervals), 2.0, 1.0)
    scaled = weights * (-1.0) ** places
    differ = points[:, None] - points[None, :] + np.eye(node_count)
    matrix = np.outer(scaled, 1.0 / scaled) / differ
    matrix = matrix - np.eye(node_count) * np.sum(matrix, axis=1)[:, None]
    return matrix / (node_count * node_count / 4.0)


def taylor_weight(degree):
    return time_step ** (degree + 1) / math.factorial(degree + 1)


def tables():
    slope = cheb_table(P_SIZE).astype(np.float32).astype(np.float64)
    high = slope.astype(ml_dtypes.bfloat16).astype(np.float64)
    low = slope - high
    one = np.eye(P_SIZE)
    two = np.eye(2)

    def spread(matrix):
        along_b = np.kron(two, np.kron(matrix.T, one))
        along_e = np.kron(two, np.kron(one, matrix.T))
        return along_b, along_e

    hy, hz = spread(high)
    ly, lz = spread(low)
    none = np.zeros_like(hy)
    w1 = np.concatenate(
        [np.concatenate([hy, hz], 1), np.concatenate([hy, hz], 1), np.concatenate([ly, lz], 1)], 0
    )
    diag_high = np.block([[hy, none], [none, hz]])
    diag_low = np.block([[ly, none], [none, lz]])
    w2 = np.concatenate([diag_high, diag_high, diag_low], 0)

    lane_half = np.arange(LANES) // HALF
    rows = []
    for t in range(TILES):
        for s in range(TILES):
            for source in (lane_half, 1 - lane_half):
                rows.append(slope[2 * t + lane_half, 2 * s + source])
    xc = np.broadcast_to(np.stack(rows)[:, None, :], (len(rows), SUB, LANES))
    return (
        jnp.asarray(w1.astype(ml_dtypes.bfloat16)),
        jnp.asarray(w2.astype(ml_dtypes.bfloat16)),
        jnp.asarray(np.ascontiguousarray(xc).astype(np.float32)),
    )


def face_tables():
    node = np.arange(P_SIZE**3)
    places = (node // P_SIZE % P_SIZE, node % P_SIZE)
    others = (node // HALF * P_SIZE + node % P_SIZE, node // P_SIZE)
    pick = np.zeros((P_SIZE**3, 2 * LANES))
    for k in range(2):
        for side, place in enumerate((0, P_SIZE - 1)):
            on = places[k] == place
            pick[node[on], k * LANES + side * HALF + others[k][on]] = 1.0
    squeeze = np.concatenate([pick, pick], 0).astype(ml_dtypes.bfloat16)
    spread = np.concatenate([pick.T, pick.T], 0).astype(ml_dtypes.bfloat16)
    return jnp.asarray(squeeze), jnp.asarray(spread)


def roll(value, by):
    by = by % LANES
    return value if by == 0 else pltpu.roll(value, by, value.ndim - 1)


def lane_ids(rows):
    return lax.broadcasted_iota(jnp.int32, (rows, LANES), 1)


def split(value):
    high = value.astype(jnp.bfloat16)
    return high, (value - high.astype(jnp.float32)).astype(jnp.bfloat16)


def x_slopes(load, turned, rows, slopes, xc_ref):
    for i, f in enumerate(along_x):
        for t in range(TILES):
            turned[i, :, span(t)] = roll(load(f, 0, rows, t), HALF)
    for i, f in enumerate(along_x):
        for r in range(0, rows, SUB):
            at = pl.ds(r, SUB)
            own = [load(f, r, SUB, t) for t in range(TILES)]
            other = [turned[i, at, span(t)] for t in range(TILES)]
            for t in range(TILES):
                total = None
                for s in range(TILES):
                    for swap, source in enumerate((own[s], other[s])):
                        term = source * xc_ref[(t * TILES + s) * 2 + swap]
                        total = term if total is None else total + term
                slopes[i, at, span(t)] = total


def begin_operator(load, parts, tabs, scratch, rows):
    w1_ref, w2_ref, xc_ref = tabs
    a1, a2, o1, o2, turned, slopes = scratch
    for i, f in enumerate(both_yz):
        for t in range(TILES):
            high, low = parts(f, t)
            at = pl.ds((i * TILES + t) * rows, rows)
            a1[at, 0:LANES] = high
            a1[at, LANES : 2 * LANES] = low
            a1[at, 2 * LANES : 3 * LANES] = high
    for i, pair in enumerate(pairs_yz):
        for t in range(TILES):
            at = pl.ds((i * TILES + t) * rows, rows)
            for place, f in enumerate(pair):
                high, low = parts(f, t)
                for block, piece in ((0, high), (2, low), (4, high)):
                    column = (block + place) * LANES
                    a2[at, column : column + LANES] = piece
    o1[...] = jnp.dot(a1[...], w1_ref[...], preferred_element_type=jnp.float32)
    o2[...] = jnp.dot(a2[...], w2_ref[...], preferred_element_type=jnp.float32)
    x_slopes(load, turned, rows, slopes, xc_ref)


def end_operator(material, scratch, rows, scale, emit):
    _, _, o1, o2, _, slopes = scratch

    def yz(ref, i, t, r):
        at = pl.ds((i * TILES + t) * rows + r, SUB)
        return ref[at, 0:LANES], ref[at, LANES : 2 * LANES]

    for r in range(0, rows, SUB):
        factor = scale(r)
        for t in range(TILES):
            lame, shear, light = [m if factor is None else m * factor for m in material(r, t)]
            shear_2 = shear + shear
            dy_vx, dz_vx = yz(o1, 0, t, r)
            dy_vy, dz_vy = yz(o1, 1, t, r)
            dy_vz, dz_vz = yz(o1, 2, t, r)
            dy_syz, dz_syz = yz(o1, 3, t, r)
            dy_syy, dz_szz = yz(o2, 0, t, r)
            dy_sxy, dz_sxz = yz(o2, 1, t, r)
            dx_vx, dx_vy, dx_vz, dx_sxx, dx_sxy, dx_sxz = (
                slopes[i, pl.ds(r, SUB), span(t)] for i in range(6)
            )
            diverge = lame * (dx_vx + dy_vy + dz_vz)
            emit(0, r, t, diverge + shear_2 * dx_vx)
            emit(1, r, t, diverge + shear_2 * dy_vy)
            emit(2, r, t, diverge + shear_2 * dz_vz)
            emit(3, r, t, shear * (dy_vx + dx_vy))
            emit(4, r, t, shear * (dz_vy + dy_vz))
            emit(5, r, t, shear * (dz_vx + dx_vz))
            emit(6, r, t, light * (dx_sxx + dy_sxy + dz_sxz))
            emit(7, r, t, light * (dx_sxy + dy_syy + dz_syz))
            emit(8, r, t, light * (dx_sxz + dy_syz + dz_szz))


def apply_operator(load, split_rows, material, tabs, scratch, rows, scale, emit):
    groups = len(scratch) // OPERATOR_SCRATCH
    size = rows // groups
    parts = [scratch[g * OPERATOR_SCRATCH : (g + 1) * OPERATOR_SCRATCH] for g in range(groups)]
    for g in range(groups):
        first = g * size
        begin_operator(
            lambda f, r, count, t: load(f, first + r, count, t),
            lambda f, t: split_rows(f, first, size, t),
            tabs,
            parts[g],
            size,
        )
    for g in range(groups):
        first = g * size
        end_operator(
            lambda r, t: material(first + r, t),
            parts[g],
            size,
            lambda r: scale(first + r),
            lambda f, r, t, value: emit(f, first + r, t, value),
        )


def span(tile):
    return slice(tile * LANES, (tile + 1) * LANES)


def pack_faces(read, rows):
    low = lane_ids(rows // 2) < HALF
    first, second = read(0, 0), read(rows // 2, 0)
    start = jnp.where(low, first, roll(second, HALF))
    first, second = read(0, 3), read(rows // 2, 3)
    end = jnp.where(low, roll(first, HALF), second)
    return end, start


def wave_speed(density, lame, shear):
    return jnp.sqrt((lame + 2.0 * shear) / density)


def early_kernel(*refs):
    sources, targets = refs[:LOADED], refs[LOADED : 2 * LOADED]
    out_ref, end_ref, start_ref = refs[2 * LOADED : 2 * LOADED + 3]
    sems, scratch = refs[2 * LOADED + 3], refs[2 * LOADED + 4 :]
    sol_ref, mat_ref, w1_ref, w2_ref, xc_ref = targets[:5]
    rows = out_ref.shape[1]
    upper, lower = pl.ds(rows, rows), pl.ds(0, rows)
    pairs = [(sources[i].at[:, upper, :], targets[i].at[:, upper, :]) for i in range(2)]
    pairs += [(sources[i], targets[i]) for i in range(2, 5)]
    pairs += [(sources[i].at[:, lower, :], targets[i].at[:, lower, :]) for i in range(2)]
    pairs += [(sources[i], targets[i]) for i in range(5, LOADED)]
    copies = [pltpu.make_async_copy(source, target, sems.at[i]) for i, (source, target) in enumerate(pairs)]
    for copy in copies:
        copy.start()
    for copy in copies[:5]:
        copy.wait()
    load = lambda f, r, count, t: sol_ref[f, rows + r : rows + r + count, span(t)]
    material = lambda r, t: (
        mat_ref[1, rows + r : rows + r + SUB, span(t)],
        mat_ref[2, rows + r : rows + r + SUB, span(t)],
        1.0 / mat_ref[0, rows + r : rows + r + SUB, span(t)],
    )

    def emit(f, r, t, value):
        base = time_step * load(f, r, SUB, t)
        out_ref[f, r : r + SUB, span(t)] = base + value

    split_rows = lambda f, r, count, t: split(load(f, r, count, t))
    tabs = (w1_ref, w2_ref, xc_ref)
    apply_operator(load, split_rows, material, tabs, scratch, rows, lambda r: taylor_weight(1), emit)
    for copy in copies[5:]:
        copy.wait()
    count = rows // 2
    for f in range(9):
        end, start = pack_faces(lambda r, t, f=f: out_ref[f, r : r + count, span(t)], rows)
        end_ref[f] = end
        start_ref[f] = start
    for i in range(2):

        def speed(r, t, i=i):
            return wave_speed(*[mat_ref[m, i * rows + r : i * rows + r + count, span(t)] for m in range(3)])

        end, start = pack_faces(speed, rows)
        end_ref[9 + i] = end
        start_ref[9 + i] = start


def refined_kernel(count_ref, sol_ref, mat_ref, w1_ref, w2_ref, xc_ref, out_ref, end_ref, start_ref, state, light, *scratch):
    rows = out_ref.shape[1]
    limit = count_ref[0, 0]
    for f in range(9):
        first = time_step * sol_ref[f, :rows, :]
        state[f] = first
        out_ref[f] = first
    light[...] = 1.0 / mat_ref[0, :rows, :]
    load = lambda f, r, count, t: state[f, r : r + count, span(t)]
    material = lambda r, t: (
        mat_ref[1, r : r + SUB, span(t)],
        mat_ref[2, r : r + SUB, span(t)],
        light[r : r + SUB, span(t)],
    )

    def emit(f, r, t, value):
        state[f, r : r + SUB, span(t)] = value
        out_ref[f, r : r + SUB, span(t)] = out_ref[f, r : r + SUB, span(t)] + value

    def term(degree, carry):
        ratio = time_step / jnp.full((SUB, LANES), degree + 1, jnp.int32).astype(jnp.float32)
        bound = jnp.where(degree < 2, rows, limit)

        def scale(r):
            ids = r + lax.broadcasted_iota(jnp.int32, (SUB, LANES), 0)
            return jnp.where(ids < bound, ratio, 0.0)

        split_rows = lambda f, r, count, t: split(state[f, r : r + count, span(t)])
        tabs = (w1_ref, w2_ref, xc_ref)
        apply_operator(load, split_rows, material, tabs, scratch, rows, scale, emit)
        return carry

    lax.fori_loop(1, ORD, term, 0)
    count = rows // 2
    for f in range(9):
        end, start = pack_faces(lambda r, t, f=f: out_ref[f, r : r + count, span(t)], rows)
        end_ref[f] = end
        start_ref[f] = start


def hot(row, first, count):
    cells = row.shape[1]
    ids = first + lax.broadcasted_iota(jnp.int32, (count, cells), 0)
    return jnp.where(ids == row, 1.0, 0.0).T


def hot_back(row):
    cells = row.shape[1]
    ids = lax.broadcasted_iota(jnp.int32, (cells, cells), 0)
    return jnp.where(ids == row, 1.0, 0.0).astype(jnp.bfloat16)


def unpack_faces(after, before):
    low = lane_ids(after.shape[0]) < HALF
    return jnp.concatenate(
        [
            jnp.where(low, after, 0.0),
            jnp.where(low, roll(after, HALF), 0.0),
            jnp.where(low, 0.0, roll(before, HALF)),
            jnp.where(low, 0.0, before),
        ],
        0,
    )


def flux(direction, jump, lame, shear, light, speed):
    members = ((6, 7, 8, 0, 3, 5), (6, 7, 8, 3, 1, 4), (6, 7, 8, 5, 4, 2))[direction]
    g = [jump[m] for m in members]
    through = g[direction]
    spread_out = lame * through
    normal = [spread_out, spread_out, spread_out, None, None, None, light * g[3], light * g[4], light * g[5]]
    normal[direction] = spread_out + 2.0 * (shear * through)
    if direction == 0:
        normal[3], normal[5] = shear * g[1], shear * g[2]
    elif direction == 1:
        normal[3], normal[4] = shear * g[0], shear * g[2]
    else:
        normal[4], normal[5] = shear * g[1], shear * g[0]
    return [
        speed * jump[f] if normal[f] is None else normal[f] + speed * jump[f] for f in range(9)
    ]


def correct_kernel(
    sol_ref, mat_ref, low_ref, high_ref, near_ref, after_ref, before_ref,
    w1_ref, w2_ref, xc_ref, squeeze_ref, spread_ref,
    out_ref, ends_ref, xmat_ref, late_ref,
    pieces, compact, xfix, hot_ref, rhs, far, fix, fixed, light, fixes, middle, sems, *scratch,
):
    cells = sol_ref.shape[1]
    half = low_ref.shape[1]
    nodes = sol_ref.shape[2]
    in_low = lane_ids(SUB) < HALF
    all_low = lane_ids(cells) < HALF
    side = jnp.where(in_low, 0.25, -0.25)

    def integral(f, r, count, t):
        if r < half:
            return low_ref[f, r : r + count, span(t)]
        return high_ref[f, r - half : r - half + count, span(t)]

    for f in range(12):
        for start in (0, half):
            at = pl.ds(f * cells + start, half)
            for t in range(TILES):
                value = integral(f, start, half, t) if f < 9 else mat_ref[f - 9, start : start + half, span(t)]
                high, low = split(value)
                pieces[at, span(t)] = high
                pieces[at, nodes + t * LANES : nodes + (t + 1) * LANES] = low
    for f in range(0, 12, 3):
        at = pl.ds(f * cells, 3 * cells)
        compact[at, :] = jnp.dot(pieces[at, :], squeeze_ref[...], preferred_element_type=jnp.float32)
    light[...] = 1.0 / mat_ref[0]

    here = near_ref[...] % cells
    for k in range(2):
        direction = k + 1
        plus = hot_back(here[2 * direction : 2 * direction + 1])
        minus = hot_back(here[2 * direction + 1 : 2 * direction + 2])
        for i in range(2):
            hot_ref[k, :, 2 * i * LANES : (2 * i + 1) * LANES] = plus
            hot_ref[k, :, (2 * i + 1) * LANES : (2 * i + 2) * LANES] = minus

        def face(f, k=k):
            return compact[pl.ds(f * cells, cells), span(k)]

        for f in range(10):
            own = face(f) if f < 9 else wave_speed(face(9), face(10), face(11))
            if f == 9:
                far[k, :, span(10)] = own
            turned = roll(own, HALF)
            for i, piece in enumerate((jnp.where(all_low, turned, 0.0), jnp.where(all_low, 0.0, turned))):
                high, low = split(piece)
                rhs[k, i * LANES : (i + 1) * LANES, span(f)] = high
                rhs[k, (i + 2) * LANES : (i + 3) * LANES, span(f)] = low
        far[k, :, : 10 * LANES] = jnp.dot(hot_ref[k], rhs[k], preferred_element_type=jnp.float32)
        for r in range(0, cells, SUB):
            at = pl.ds(r, SUB)

            def own(f, k=k, r=r):
                return compact[pl.ds(f * cells + r, SUB), span(k)]

            jump = [far[k, at, span(f)] - own(f) for f in range(9)]
            speed = 0.25 * jnp.maximum(far[k, at, span(9)], far[k, at, span(10)])
            values = flux(direction, jump, side * own(10), side * own(11), side / own(9), speed)
            for f, value in enumerate(values):
                fix[pl.ds(f * cells + r, SUB), span(k)] = value
    for f in range(9):
        at = pl.ds(f * cells, cells)
        for k in range(2):
            high, low = split(fix[at, span(k)])
            fixed[at, span(k)] = high
            fixed[at, span(k + 2)] = low

    plus, minus = here[1:2], here[0:1]
    plus, minus = hot(plus, 0, cells), hot(minus, 0, cells)
    early = jnp.concatenate([plus[:, half:], minus[:, half:]], 1).astype(jnp.bfloat16)
    late = jnp.concatenate([plus[:, :half], minus[:, :half]], 1).astype(jnp.bfloat16)
    late_ref[:, :LANES] = late
    late_ref[:, LANES:] = late
    hot_ref[2, :, 0 * LANES : 1 * LANES] = early
    hot_ref[2, :, 1 * LANES : 2 * LANES] = early
    hot_ref[2, :, 2 * LANES : 3 * LANES] = late
    hot_ref[2, :, 3 * LANES : 4 * LANES] = late
    for f in range(9):
        high, low = split(unpack_faces(after_ref[f], before_ref[f]))
        rhs[2, 0:LANES, span(f)] = high
        rhs[2, LANES : 2 * LANES, span(f)] = low
    for k, f in ((0, 10), (2, 9)):
        high, low = split(unpack_faces(after_ref[f], before_ref[f]))
        rhs[2, k * LANES : (k + 1) * LANES, span(9)] = high
        rhs[2, (k + 1) * LANES : (k + 2) * LANES, span(9)] = low
    far[2, :, : 9 * LANES] = jnp.dot(
        hot_ref[2, :, : 2 * LANES], rhs[2, : 2 * LANES, : 9 * LANES], preferred_element_type=jnp.float32
    )
    far[2, :, span(9)] = jnp.dot(hot_ref[2], rhs[2, :, span(9)], preferred_element_type=jnp.float32)
    for r in range(0, cells, SUB):
        at = pl.ds(r, SUB)
        jump = [
            far[2, at, span(f)] - jnp.where(in_low, integral(f, r, SUB, 0), integral(f, r, SUB, 3)) for f in range(9)
        ]
        density, lame, shear = (
            jnp.where(in_low, mat_ref[m, at, span(0)], mat_ref[m, at, span(3)]) for m in range(3)
        )
        speed = 0.25 * jnp.maximum(far[2, at, span(9)], wave_speed(density, lame, shear))
        lame, shear, weight = side * lame, side * shear, side / density
        for f, value in enumerate(flux(0, jump, lame, shear, weight, speed)):
            xfix[f, at, :] = value
        for i, value in enumerate((lame, shear, weight, speed)):
            xmat_ref[i, at, :] = value

    for f in range(0, 9, 3):
        at = pl.ds(f * cells, 3 * cells)
        fixes[at, :] = jnp.dot(fixed[at, :], spread_ref[...], preferred_element_type=jnp.float32)

    def split_rows(f, r, count, t):
        at = pl.ds(f * cells + r, count)
        return pieces[at, span(t)], pieces[at, nodes + t * LANES : nodes + (t + 1) * LANES]

    def material(r, t):
        at = pl.ds(r, SUB)
        return mat_ref[1, at, span(t)], mat_ref[2, at, span(t)], light[at, span(t)]

    def emit(f, r, t, value):
        at = pl.ds(r, SUB)
        total = sol_ref[f, at, span(t)] + value + fixes[pl.ds(f * cells + r, SUB), span(t)]
        if t == 0:
            ends_ref[0, f, at, :] = total + jnp.where(in_low, xfix[f, at, :], 0.0)
        elif t == TILES - 1:
            ends_ref[1, f, at, :] = total + jnp.where(in_low, 0.0, xfix[f, at, :])
        else:
            middle[f, at, span(t - 1)] = total
        if f == 8 and t == TILES - 1 and (r + SUB) % half == 0:
            stores[r // half].start()

    between = pl.ds(LANES, (TILES - 2) * LANES)
    stores = [
        pltpu.make_async_copy(
            middle.at[:, pl.ds(start, half), :], out_ref.at[:, pl.ds(start, half), between], sems.at[i]
        )
        for i, start in enumerate(range(0, cells, half))
    ]
    tabs = (w1_ref, w2_ref, xc_ref)
    apply_operator(integral, split_rows, material, tabs, scratch, cells, lambda r: None, emit)
    for copy in stores:
        copy.wait()


def finish_kernel(done_ref, ends_ref, after_ref, before_ref, xmat_ref, late_ref, out_ref, ends, rhs, far, sems):
    del done_ref
    cells = ends.shape[2]
    for f in range(9):
        high, low = split(unpack_faces(after_ref[f], before_ref[f]))
        rhs[0:LANES, span(f)] = high
        rhs[LANES : 2 * LANES, span(f)] = low
    for f in range(0, 9, 3):
        columns = slice(f * LANES, (f + 3) * LANES)
        far[:, columns] = jnp.dot(late_ref[...], rhs[:, columns], preferred_element_type=jnp.float32)
    in_low = lane_ids(SUB) < HALF
    size = cells // sems.shape[1]
    stores = []
    for r in range(0, cells, SUB):
        at = pl.ds(r, SUB)
        jump = [far[at, span(f)] for f in range(9)]
        lame, shear, weight, speed = (xmat_ref[i, at, :] for i in range(4))
        for f, value in enumerate(flux(0, jump, lame, shear, weight, speed)):
            ends[0, f, at, :] = ends_ref[0, f, at, :] + jnp.where(in_low, value, 0.0)
            ends[1, f, at, :] = ends_ref[1, f, at, :] + jnp.where(in_low, 0.0, value)
        if (r + SUB) % size == 0:
            part = pl.ds(r + SUB - size, size)
            for i, t in enumerate((0, TILES - 1)):
                copy = pltpu.make_async_copy(
                    ends.at[i, :, part, :], out_ref.at[:, part, pl.ds(t * LANES, LANES)], sems.at[i, r // size]
                )
                copy.start()
                stores.append(copy)
    for copy in stores:
        copy.wait()


def shifted(value, axis, by):
    peers = lax.axis_size(axis)
    return lax.ppermute(value, axis, [(i, (i + by) % peers) for i in range(peers)])


def f32(*shape):
    return jax.ShapeDtypeStruct(shape, jnp.float32)


def operator_scratch(rows):
    return [
        pltpu.VMEM((len(both_yz) * TILES * rows, 3 * LANES), jnp.bfloat16),
        pltpu.VMEM((len(pairs_yz) * TILES * rows, 6 * LANES), jnp.bfloat16),
        pltpu.VMEM((len(both_yz) * TILES * rows, 2 * LANES), jnp.float32),
        pltpu.VMEM((len(pairs_yz) * TILES * rows, 2 * LANES), jnp.float32),
        pltpu.VMEM((len(along_x), rows, TILES * LANES), jnp.float32),
        pltpu.VMEM((len(along_x), rows, TILES * LANES), jnp.float32),
    ]


def on_device(solution, material, neighbours, refine_count):
    cells, nodes = solution.shape[1:]
    rows = REF_MAX
    params = lambda mib: pltpu.CompilerParams(vmem_limit_bytes=mib * 1024 * 1024)
    early_shape, late_shape = (11, rows // 2, LANES), (9, rows // 2, LANES)
    in_vmem = pl.BlockSpec(memory_space=pltpu.VMEM)
    in_hbm = pl.BlockSpec(memory_space=pltpu.HBM)
    in_smem = pl.BlockSpec(memory_space=pltpu.SMEM)
    operator = operator_scratch(rows // 2) * 2

    sources = (solution, material) + tables() + face_tables()
    *loaded, high, end, start = pl.pallas_call(
        early_kernel,
        in_specs=[in_hbm] * LOADED,
        out_specs=[in_vmem] * (LOADED + 3),
        out_shape=[pltpu.VMEM(x.shape, x.dtype) for x in sources]
        + [pltpu.VMEM((9, rows, nodes), jnp.float32), f32(*early_shape), f32(*early_shape)],
        scratch_shapes=[pltpu.SemaphoreType.DMA((LOADED + 2,))] + operator,
        compiler_params=params(20),
        name="early",
    )(*[pltpu.with_memory_space_constraint(x, pltpu.HBM) for x in sources])
    sol, mat, w1, w2, xc, squeeze, spread = loaded
    early_after = shifted(end, "space", -1)
    early_before = shifted(start, "space", 1)

    low, end, start = pl.pallas_call(
        refined_kernel,
        in_specs=[in_smem] + [in_vmem] * 5,
        out_specs=[in_vmem] * 3,
        out_shape=[pltpu.VMEM((9, rows, nodes), jnp.float32), f32(*late_shape), f32(*late_shape)],
        scratch_shapes=[
            pltpu.VMEM((9, rows, nodes), jnp.float32),
            pltpu.VMEM((rows, nodes), jnp.float32),
        ]
        + operator,
        compiler_params=params(20),
        name="refined",
    )(refine_count, sol, mat, w1, w2, xc)
    late_after = shifted(end, "space", -1)
    late_before = shifted(start, "space", 1)

    done, ends, xmat, late_hot = pl.pallas_call(
        correct_kernel,
        in_specs=[in_vmem] * 12,
        out_specs=[in_hbm] + [in_vmem] * 3,
        out_shape=[
            pltpu.HBM(solution.shape, jnp.float32),
            pltpu.VMEM((2, 9, cells, LANES), jnp.float32),
            pltpu.VMEM((4, cells, LANES), jnp.float32),
            pltpu.VMEM((cells, 2 * LANES), jnp.bfloat16),
        ],
        scratch_shapes=[
            pltpu.VMEM((12 * cells, 2 * nodes), jnp.bfloat16),
            pltpu.VMEM((12 * cells, 2 * LANES), jnp.float32),
            pltpu.VMEM((9, cells, LANES), jnp.float32),
            pltpu.VMEM((3, cells, 4 * LANES), jnp.bfloat16),
            pltpu.VMEM((3, 4 * LANES, 10 * LANES), jnp.bfloat16),
            pltpu.VMEM((3, cells, 11 * LANES), jnp.float32),
            pltpu.VMEM((9 * cells, 2 * LANES), jnp.float32),
            pltpu.VMEM((9 * cells, 4 * LANES), jnp.bfloat16),
            pltpu.VMEM((cells, nodes), jnp.float32),
            pltpu.VMEM((9 * cells, nodes), jnp.float32),
            pltpu.VMEM((9, cells, nodes - 2 * LANES), jnp.float32),
            pltpu.SemaphoreType.DMA((2,)),
        ]
        + operator_scratch(rows) * 2,
        compiler_params=params(40),
        name="correct",
    )(sol, mat, low, high, neighbours, early_after, early_before, w1, w2, xc, squeeze, spread)

    return pl.pallas_call(
        finish_kernel,
        in_specs=[in_hbm] + [in_vmem] * 5,
        out_specs=in_hbm,
        out_shape=f32(*solution.shape),
        scratch_shapes=[
            pltpu.VMEM((2, 9, cells, LANES), jnp.float32),
            pltpu.VMEM((2 * LANES, 9 * LANES), jnp.bfloat16),
            pltpu.VMEM((cells, 9 * LANES), jnp.float32),
            pltpu.SemaphoreType.DMA((2, 4)),
        ],
        input_output_aliases={0: 0},
        compiler_params=params(8),
        name="finish",
    )(done, ends, late_after, late_before, xmat, late_hot)


def solution(mesh):
    in_specs = (
        P(None, ("space", "help"), None),
        P(None, ("space", "help"), None),
        P(None, ("space", "help")),
        P("space", "help"),
    )
    out_specs = P(None, ("space", "help"), None)
    return jax.shard_map(
        on_device, mesh=mesh, in_specs=in_specs, out_specs=out_specs, check_vma=False
    )
```

time: 69 us -> 25.4 us (0.37)
  Pallas kernels: 60.7 us -> 18.4 us
  local copies, waits for them, and re-layouts: 1.44 us -> 0.01 us
    pallas_call x4, Pallas kernels: 60.7 us -> 18.4 us  [the longest x1 7.99 us: on_device(): pl.pallas_call(refined_kernel, in_specs=[in_smem] + [in_vmem] * 5, out_sp...]
    unnamed x8 -> x2, local copies, waits for them, and re-layouts: 1.44 us -> 0.01 us
  transfers between devices with their start and end apart: 4 -> 4, of which waited for: 0 -> 0; matrix products, arithmetic and copies ran while one was open for 0% -> 0% of each run, Pallas kernels for 72% -> 55%
where the time goes in v2:
time: 25.4 us; the launch traced here: 25.2 us
  Pallas kernels  18.4 us (72%)
  starting transfers between devices  6.09 us (24%)
  between operations  0.71 us (3%)
    pallas_call x1, Pallas kernels, on_device(): pl.pallas_call(refined_kernel, in_specs=[in_smem] + [in_vmem] * 5, out_sp...  7.99 us
    ppermute x4, starting transfers between devices, shifted(): lax.ppermute(value, axis, [(i, (i + by) % peers) for i in range(peers)])  6.09 us
    pallas_call x1, Pallas kernels, on_device(): pl.pallas_call(correct_kernel, in_specs=[in_vmem] * 12, out_specs=[in_hbm...  5.99 us
    pallas_call x1, Pallas kernels, on_device(): pl.pallas_call(early_kernel, in_specs=[in_hbm] * LOADED, out_specs=[in_vm...  2.98 us
    pallas_call x1, Pallas kernels, on_device(): pl.pallas_call(finish_kernel, in_specs=[in_hbm] + [in_vmem] * 5, out_spec...  1.45 us
  transfers between devices with their start and end apart: 4, of which 0 were waited for; matrix products, arithmetic and copies ran while one was open for 0% of the time, Pallas kernels for 55%

profile of v2, /device:TPU:0, one launch (start us, length us, event | category | flops | bytes accessed | tf_op | source)
XLA Modules:
  0.0 25.2 jit_solution(298257072785600740)
XLA Ops:
  0.0 3.0 %early.1 = (f32[9,128,512]{2,1,0:T(8,128)S(1)}, f32[3,128,512]{2,1,0:T(8,128)S(1)}, bf16[384,256]{1,0:T(8,128)(2,1)S(1)}, bf16[768,256]{1,0:T(8,128)(2,1)S(1)}, ...) custom-call(f32[9,128,512]{2,1,0:T(8,128)} %refs_0_.1, ...), custom_call_target="tpu_custom_call" | custom-call | tf_op jit(solution)/shard_map/early/pallas_call | solution.py:563
  3.0 0.0 copy-start
  3.0 3.4 %collective-permute-start = (f32[11,32,128]{2,1,0:T(8,128)S(1)}, f32[11,32,128]{2,1,0:T(8,128)S(1)}, u32[]{:S(2)}, u32[]{:S(2)}) collective-permute-start(f32[11,32,128]{2,1,0:T(8,128)S(1)} %get-tuple-element.29), channel_id=1, source_target_pairs={{0,28},{4,0},{8,4},{12,8},{16,12},{20,16},{24,20},{28,24},{1,29},{... | collective-permute-start | bytes 540680 | tf_op jit(solution)/shard_map/ppermute | solution.py:534
  6.4 0.0 collective-permute-start.1
  7.0 8.0 %refined.1 = (f32[9,64,512]{2,1,0:T(8,128)S(1)}, f32[9,32,128]{2,1,0:T(8,128)S(1)}, f32[9,32,128]{2,1,0:T(8,128)S(1)}) custom-call(s32[1,1]{1,0:T(1,128)S(6)} %copy.12.count_ref, f32[9,128,512]{2,1,0:T(8,128)S(1)} %get-tuple-element.22.sol_ref, f32[3,128,512]{2,1,0:T(8,128)S(1)} %get-tuple-element.23.mat_ref, bf16[384,256]{1,0:T(8,128)(2,1)S(1)} %get-tuple-element.24.w1_ref, ...), custom_call_target="tpu_custom_call" | custom-call | tf_op jit(solution)/shard_map/refined/pallas_call | solution.py:577
  15.0 2.7 %collective-permute-start.2 = (f32[9,32,128]{2,1,0:T(8,128)S(1)}, f32[9,32,128]{2,1,0:T(8,128)S(1)}, u32[]{:S(2)}, u32[]{:S(2)}) collective-permute-start(f32[9,32,128]{2,1,0:T(8,128)S(1)} %get-tuple-element.35), channel_id=1, source_target_pairs={{0,28},{4,0},{8,4},{12,8},{16,12},{20,16},{24,20},{28,24},{1,29},{... | collective-permute-start | bytes 442376 | tf_op jit(solution)/shard_map/ppermute | solution.py:534
  17.7 0.0 collective-permute-start.3
  17.7 0.0 collective-permute-done.after_ref
  17.7 0.0 collective-permute-done.1.before_ref
  17.7 0.0 copy-done
  17.8 6.0 %correct.1 = (f32[9,128,512]{2,1,0:T(8,128)}, f32[2,9,128,128]{3,2,1,0:T(8,128)S(1)}, f32[4,128,128]{2,1,0:T(8,128)S(1)}, bf16[128,256]{1,0:T(8,128)(2,1)S(1)}) custom-call(f32[9,128,512]{2,1,0:T(8,128)S(1)} %get-tuple-element.22.sol_ref, f32[3,128,512]{2,1,0:T(8,128)S(1)} %get-tuple-element.23.mat_ref, f32[9,64,512]{2,1,0:T(8,128)S(1)} %get-tuple-element.27.low_ref, ...), custom_call_target="tpu_custom_call" | custom-call | tf_op jit(solution)/shard_map/correct/pallas_call | solution.py:593
  23.8 0.0 collective-permute-done.2.after_ref
  23.8 0.0 collective-permute-done.3.before_ref
  23.8 1.4 %finish.1 = f32[9,128,512]{2,1,0:T(8,128)} custom-call(f32[9,128,512]{2,1,0:T(8,128)} %get-tuple-element.33.done_ref, f32[2,9,128,128]{3,2,1,0:T(8,128)S(1)} %get-tuple-element.34.ends_ref, f32[9,32,128]{2,1,0:T(8,128)S(1)} %collective-permute-done.2.after_ref, f32[9,32,128]{2,1,0:T(8,128)S(1)} %collective-permute-done.3.before_ref, ...), custom_call_target="tpu_custom_call", output_to_operand_aliasing={{}: (0, {})} | custom-call | tf_op jit(solution)/shard_map/finish/pallas_call | solution.py:622
Async XLA Ops:
  3.0 14.8 %copy-start = (s32[6,128]{1,0:T(8,128)S(1)}, s32[6,128]{1,0:T(8,128)}, u32[]{:S(2)}) copy-start(s32[6,128]{1,0:T(8,128)} %near_ref.1) | copy-start | bytes 9220
  3.0 14.7 %collective-permute-start = (f32[11,32,128]{2,1,0:T(8,128)S(1)}, f32[11,32,128]{2,1,0:T(8,128)S(1)}, u32[]{:S(2)}, u32[]{:S(2)}) collective-permute-start(f32[11,32,128]{2,1,0:T(8,128)S(1)} %get-tuple-element.29), channel_id=1, source_target_pairs={{0,28},{4,0},{8,4},{12,8},{16,12},{20,16},{24,20},{28,24},{1,29},{... | collective-permute-start | bytes 540680 | tf_op jit(solution)/shard_map/ppermute | solution.py:534
  6.4 11.4 %collective-permute-start.1 = (f32[11,32,128]{2,1,0:T(8,128)S(1)}, f32[11,32,128]{2,1,0:T(8,128)S(1)}, u32[]{:S(2)}, u32[]{:S(2)}) collective-permute-start(f32[11,32,128]{2,1,0:T(8,128)S(1)} %get-tuple-element.30), channel_id=1, source_target_pairs={{0,4},{4,8},{8,12},{12,16},{16,20},{20,24},{24,28},{28,0},{1,5},{5... | collective-permute-start | bytes 540680 | tf_op jit(solution)/shard_map/ppermute | solution.py:534
  15.0 8.7 %collective-permute-start.2 = (f32[9,32,128]{2,1,0:T(8,128)S(1)}, f32[9,32,128]{2,1,0:T(8,128)S(1)}, u32[]{:S(2)}, u32[]{:S(2)}) collective-permute-start(f32[9,32,128]{2,1,0:T(8,128)S(1)} %get-tuple-element.35), channel_id=1, source_target_pairs={{0,28},{4,0},{8,4},{12,8},{16,12},{20,16},{24,20},{28,24},{1,29},{... | collective-permute-start | bytes 442376 | tf_op jit(solution)/shard_map/ppermute | solution.py:534
  17.7 6.0 %collective-permute-start.3 = (f32[9,32,128]{2,1,0:T(8,128)S(1)}, f32[9,32,128]{2,1,0:T(8,128)S(1)}, u32[]{:S(2)}, u32[]{:S(2)}) collective-permute-start(f32[9,32,128]{2,1,0:T(8,128)S(1)} %get-tuple-element.36), channel_id=1, source_target_pairs={{0,4},{4,8},{8,12},{12,16},{16,20},{20,24},{24,28},{28,0},{1,5},{5... | collective-permute-start | bytes 442376 | tf_op jit(solution)/shard_map/ppermute | solution.py:534

commit v3 on v2

--- a/solution.py
+++ b/solution.py
@@ -16,7 +16,7 @@
 TILES = 4
 HALF = 64
 SUB = 8
-OPERATOR_SCRATCH = 6
+PACK = 16
 LOADED = 7
 
 along_x = (6, 7, 8, 0, 3, 5)
@@ -65,12 +65,16 @@
     diag_low = np.block([[ly, none], [none, lz]])
     w2 = np.concatenate([diag_high, diag_high, diag_low], 0)
 
+    half = P_SIZE // 2
+    top = slope[:half, :half]
+    mirror = slope[:half, ::-1][:, :half]
     lane_half = np.arange(LANES) // HALF
     rows = []
-    for t in range(TILES):
-        for s in range(TILES):
-            for source in (lane_half, 1 - lane_half):
-                rows.append(slope[2 * t + lane_half, 2 * s + source])
+    for part in ((top + mirror) / 2, (top - mirror) / 2):
+        for t in range(2):
+            for s in range(2):
+                for source in (lane_half, 1 - lane_half):
+                    rows.append(part[2 * t + lane_half, 2 * s + source])
     xc = np.broadcast_to(np.stack(rows)[:, None, :], (len(rows), SUB, LANES))
     return (
         jnp.asarray(w1.astype(ml_dtypes.bfloat16)),
@@ -82,14 +86,24 @@
 def face_tables():
     node = np.arange(P_SIZE**3)
     places = (node // P_SIZE % P_SIZE, node % P_SIZE)
-    others = (node // HALF * P_SIZE + node % P_SIZE, node // P_SIZE)
+    others = (
+        node // HALF * P_SIZE + node % P_SIZE,
+        (node // HALF + P_SIZE // 2) % P_SIZE * P_SIZE + node // P_SIZE % P_SIZE,
+    )
     pick = np.zeros((P_SIZE**3, 2 * LANES))
     for k in range(2):
         for side, place in enumerate((0, P_SIZE - 1)):
             on = places[k] == place
             pick[node[on], k * LANES + side * HALF + others[k][on]] = 1.0
     squeeze = np.concatenate([pick, pick], 0).astype(ml_dtypes.bfloat16)
-    spread = np.concatenate([pick.T, pick.T], 0).astype(ml_dtypes.bfloat16)
+    in_first = np.arange(LANES) % HALF < HALF // 2
+    both = []
+    for part in range(2):
+        keep_y = in_first if part == 0 else ~in_first
+        mixed = np.where(keep_y[None, :], pick[:, :LANES], pick[:, LANES:])
+        piece = mixed[part * 2 * LANES : (part + 1) * 2 * LANES].T
+        both += [piece, piece]
+    spread = np.concatenate(both, 0).astype(ml_dtypes.bfloat16)
     return jnp.asarray(squeeze), jnp.asarray(spread)
 
 
@@ -107,68 +121,80 @@
     return high, (value - high.astype(jnp.float32)).astype(jnp.bfloat16)
 
 
-def x_slopes(load, turned, rows, slopes, xc_ref):
-    for i, f in enumerate(along_x):
+def turn(load, r):
+    return [[roll(load(f, r, SUB, t), HALF) for t in range(TILES)] for f in along_x]
+
+
+def x_slope(own, other, xc_ref):
+    sums = [[], []]
+    for kind in range(2):
+        sources = []
+        for s in range(2):
+            if kind == 0:
+                sources.append((own[s] + other[3 - s], other[s] + own[3 - s]))
+            else:
+                sources.append((own[s] - other[3 - s], other[s] - own[3 - s]))
+        for t in range(2):
+            total = None
+            for s in range(2):
+                for swap in range(2):
+                    term = sources[s][swap] * xc_ref[((kind * 2 + t) * 2 + s) * 2 + swap]
+                    total = term if total is None else total + term
+            sums[kind].append(total)
+    slopes = [None] * TILES
+    for t in range(2):
+        even, odd = sums[0][t], sums[1][t]
+        slopes[t] = even + odd
+        slopes[3 - t] = roll(odd - even, HALF)
+    return slopes
+
+
+def begin_operator(split_rows, tabs, first, rows):
+    w1_ref, w2_ref, _ = tabs
+    left, right = [], []
+    for r in range(first, first + rows, PACK):
         for t in range(TILES):
-            turned[i, :, span(t)] = roll(load(f, 0, rows, t), HALF)
-    for i, f in enumerate(along_x):
-        for r in range(0, rows, SUB):
-            at = pl.ds(r, SUB)
-            own = [load(f, r, SUB, t) for t in range(TILES)]
-            other = [turned[i, at, span(t)] for t in range(TILES)]
-            for t in range(TILES):
-                total = None
-                for s in range(TILES):
-                    for swap, source in enumerate((own[s], other[s])):
-                        term = source * xc_ref[(t * TILES + s) * 2 + swap]
-                        total = term if total is None else total + term
-                slopes[i, at, span(t)] = total
-
-
-def begin_operator(load, parts, tabs, scratch, rows):
-    w1_ref, w2_ref, xc_ref = tabs
-    a1, a2, o1, o2, turned, slopes = scratch
-    for i, f in enumerate(both_yz):
-        for t in range(TILES):
-            high, low = parts(f, t)
-            at = pl.ds((i * TILES + t) * rows, rows)
-            a1[at, 0:LANES] = high
-            a1[at, LANES : 2 * LANES] = low
-            a1[at, 2 * LANES : 3 * LANES] = high
-    for i, pair in enumerate(pairs_yz):
-        for t in range(TILES):
-            at = pl.ds((i * TILES + t) * rows, rows)
-            for place, f in enumerate(pair):
-                high, low = parts(f, t)
-                for block, piece in ((0, high), (2, low), (4, high)):
-                    column = (block + place) * LANES
-                    a2[at, column : column + LANES] = piece
-    o1[...] = jnp.dot(a1[...], w1_ref[...], preferred_element_type=jnp.float32)
-    o2[...] = jnp.dot(a2[...], w2_ref[...], preferred_element_type=jnp.float32)
-    x_slopes(load, turned, rows, slopes, xc_ref)
-
-
-def end_operator(material, scratch, rows, scale, emit):
-    _, _, o1, o2, _, slopes = scratch
-
-    def yz(ref, i, t, r):
-        at = pl.ds((i * TILES + t) * rows + r, SUB)
-        return ref[at, 0:LANES], ref[at, LANES : 2 * LANES]
-
-    for r in range(0, rows, SUB):
+            parts = {f: split_rows(f, r, PACK, t) for f in both_yz + pairs_yz[0] + pairs_yz[1]}
+            for f in both_yz:
+                high, low = parts[f]
+                left.append(jnp.concatenate([high, low, high], 1))
+            for f, g in pairs_yz:
+                (high_f, low_f), (high_g, low_g) = parts[f], parts[g]
+                right.append(jnp.concatenate([high_f, high_g, low_f, low_g, high_f, high_g], 1))
+    left, right = jnp.concatenate(left, 0), jnp.concatenate(right, 0)
+    return (
+        jnp.dot(left, w1_ref[...], preferred_element_type=jnp.float32),
+        jnp.dot(right, w2_ref[...], preferred_element_type=jnp.float32),
+    )
+
+
+def end_operator(load, material, tabs, products, first, rows, scale, emit):
+    xc_ref = tabs[2]
+    o1, o2 = products
+
+    def yz(values, count, i, t, r):
+        at = (((r - first) // PACK * TILES + t) * count + i) * PACK + r % PACK
+        return values[at : at + SUB, :LANES], values[at : at + SUB, LANES:]
+
+    following = turn(load, first)
+    for r in range(first, first + rows, SUB):
+        turned = following
+        if r + SUB < first + rows:
+            following = turn(load, r + SUB)
+        slopes = [
+            x_slope([load(f, r, SUB, t) for t in range(TILES)], turned[i], xc_ref) for i, f in enumerate(along_x)
+        ]
         factor = scale(r)
         for t in range(TILES):
             lame, shear, light = [m if factor is None else m * factor for m in material(r, t)]
             shear_2 = shear + shear
-            dy_vx, dz_vx = yz(o1, 0, t, r)
-            dy_vy, dz_vy = yz(o1, 1, t, r)
-            dy_vz, dz_vz = yz(o1, 2, t, r)
-            dy_syz, dz_syz = yz(o1, 3, t, r)
-            dy_syy, dz_szz = yz(o2, 0, t, r)
-            dy_sxy, dz_sxz = yz(o2, 1, t, r)
-            dx_vx, dx_vy, dx_vz, dx_sxx, dx_sxy, dx_sxz = (
-                slopes[i, pl.ds(r, SUB), span(t)] for i in range(6)
-            )
+            dy_vx, dz_vx = yz(o1, 4, 0, t, r)
+            dy_vy, dz_vy = yz(o1, 4, 1, t, r)
+            dy_vz, dz_vz = yz(o1, 4, 2, t, r)
+            dy_syz, dz_syz = yz(o1, 4, 3, t, r)
+            dy_syy, dz_szz = yz(o2, 2, 0, t, r)
+            dy_sxy, dz_sxz = yz(o2, 2, 1, t, r)
+            dx_vx, dx_vy, dx_vz, dx_sxx, dx_sxy, dx_sxz = (slope[t] for slope in slopes)
             diverge = lame * (dx_vx + dy_vy + dz_vz)
             emit(0, r, t, diverge + shear_2 * dx_vx)
             emit(1, r, t, diverge + shear_2 * dy_vy)
@@ -181,28 +207,11 @@
             emit(8, r, t, light * (dx_sxz + dy_syz + dz_szz))
 
 
-def apply_operator(load, split_rows, material, tabs, scratch, rows, scale, emit):
-    groups = len(scratch) // OPERATOR_SCRATCH
-    size = rows // groups
-    parts = [scratch[g * OPERATOR_SCRATCH : (g + 1) * OPERATOR_SCRATCH] for g in range(groups)]
-    for g in range(groups):
-        first = g * size
-        begin_operator(
-            lambda f, r, count, t: load(f, first + r, count, t),
-            lambda f, t: split_rows(f, first, size, t),
-            tabs,
-            parts[g],
-            size,
-        )
-    for g in range(groups):
-        first = g * size
-        end_operator(
-            lambda r, t: material(first + r, t),
-            parts[g],
-            size,
-            lambda r: scale(first + r),
-            lambda f, r, t, value: emit(f, first + r, t, value),
-        )
+def apply_operator(load, split_rows, material, tabs, rows, size, scale, emit):
+    groups = range(0, rows, size)
+    products = [begin_operator(split_rows, tabs, first, size) for first in groups]
+    for first, product in zip(groups, products):
+        end_operator(load, material, tabs, product, first, size, scale, emit)
 
 
 def span(tile):
@@ -218,14 +227,28 @@
     return end, start
 
 
+def odd_device():
+    return lax.rem(lax.axis_index("space"), 2) == 1
+
+
+def send_faces(odd, near_ref, far_ref, index, end, start):
+    near_ref[index] = jnp.where(odd, end, start)
+    far_ref[index] = jnp.where(odd, start, end)
+
+
+def got_faces(odd, near_ref, far_ref, index):
+    near, far = near_ref[index], far_ref[index]
+    return jnp.where(odd, far, near), jnp.where(odd, near, far)
+
+
 def wave_speed(density, lame, shear):
     return jnp.sqrt((lame + 2.0 * shear) / density)
 
 
 def early_kernel(*refs):
     sources, targets = refs[:LOADED], refs[LOADED : 2 * LOADED]
-    out_ref, end_ref, start_ref = refs[2 * LOADED : 2 * LOADED + 3]
-    sems, scratch = refs[2 * LOADED + 3], refs[2 * LOADED + 4 :]
+    out_ref, near_ref, far_ref = refs[2 * LOADED : 2 * LOADED + 3]
+    sems = refs[2 * LOADED + 3]
     sol_ref, mat_ref, w1_ref, w2_ref, xc_ref = targets[:5]
     rows = out_ref.shape[1]
     upper, lower = pl.ds(rows, rows), pl.ds(0, rows)
@@ -251,62 +274,63 @@
 
     split_rows = lambda f, r, count, t: split(load(f, r, count, t))
     tabs = (w1_ref, w2_ref, xc_ref)
-    apply_operator(load, split_rows, material, tabs, scratch, rows, lambda r: taylor_weight(1), emit)
+    apply_operator(load, split_rows, material, tabs, rows, rows // 2, lambda r: taylor_weight(1), emit)
     for copy in copies[5:]:
         copy.wait()
     count = rows // 2
+    odd = odd_device()
     for f in range(9):
         end, start = pack_faces(lambda r, t, f=f: out_ref[f, r : r + count, span(t)], rows)
-        end_ref[f] = end
-        start_ref[f] = start
+        send_faces(odd, near_ref, far_ref, f, end, start)
     for i in range(2):
 
         def speed(r, t, i=i):
             return wave_speed(*[mat_ref[m, i * rows + r : i * rows + r + count, span(t)] for m in range(3)])
 
         end, start = pack_faces(speed, rows)
-        end_ref[9 + i] = end
-        start_ref[9 + i] = start
-
-
-def refined_kernel(count_ref, sol_ref, mat_ref, w1_ref, w2_ref, xc_ref, out_ref, end_ref, start_ref, state, light, *scratch):
+        send_faces(odd, near_ref, far_ref, 9 + i, end, start)
+
+
+def refined_kernel(count_ref, sol_ref, mat_ref, w1_ref, w2_ref, xc_ref, out_ref, near_ref, far_ref, state, light):
     rows = out_ref.shape[1]
-    limit = count_ref[0, 0]
-    for f in range(9):
-        first = time_step * sol_ref[f, :rows, :]
-        state[f] = first
-        out_ref[f] = first
+    limit = jnp.broadcast_to(count_ref[...], (SUB, LANES))
     light[...] = 1.0 / mat_ref[0, :rows, :]
-    load = lambda f, r, count, t: state[f, r : r + count, span(t)]
+    tabs = (w1_ref, w2_ref, xc_ref)
     material = lambda r, t: (
         mat_ref[1, r : r + SUB, span(t)],
         mat_ref[2, r : r + SUB, span(t)],
         light[r : r + SUB, span(t)],
     )
 
-    def emit(f, r, t, value):
-        state[f, r : r + SUB, span(t)] = value
-        out_ref[f, r : r + SUB, span(t)] = out_ref[f, r : r + SUB, span(t)] + value
+    def next_term(source, scale, first):
+        load = lambda f, r, count, t: source[f, r : r + count, span(t)]
+        split_rows = lambda f, r, count, t: split(load(f, r, count, t))
+
+        def emit(f, r, t, value):
+            at = pl.ds(r, SUB)
+            before = time_step * sol_ref[f, at, span(t)] if first else out_ref[f, at, span(t)]
+            state[f, at, span(t)] = value
+            out_ref[f, at, span(t)] = before + value
+
+        apply_operator(load, split_rows, material, tabs, rows, rows // 2, scale, emit)
 
     def term(degree, carry):
         ratio = time_step / jnp.full((SUB, LANES), degree + 1, jnp.int32).astype(jnp.float32)
-        bound = jnp.where(degree < 2, rows, limit)
 
         def scale(r):
             ids = r + lax.broadcasted_iota(jnp.int32, (SUB, LANES), 0)
-            return jnp.where(ids < bound, ratio, 0.0)
-
-        split_rows = lambda f, r, count, t: split(state[f, r : r + count, span(t)])
-        tabs = (w1_ref, w2_ref, xc_ref)
-        apply_operator(load, split_rows, material, tabs, scratch, rows, scale, emit)
+            return jnp.where(ids < limit, ratio, 0.0)
+
+        next_term(state, scale, False)
         return carry
 
-    lax.fori_loop(1, ORD, term, 0)
+    next_term(sol_ref, lambda r: taylor_weight(1), True)
+    lax.fori_loop(2, ORD, term, 0)
     count = rows // 2
+    odd = odd_device()
     for f in range(9):
         end, start = pack_faces(lambda r, t, f=f: out_ref[f, r : r + count, span(t)], rows)
-        end_ref[f] = end
-        start_ref[f] = start
+        send_faces(odd, near_ref, far_ref, f, end, start)
 
 
 def hot(row, first, count):
@@ -353,16 +377,17 @@
 
 
 def correct_kernel(
-    sol_ref, mat_ref, low_ref, high_ref, near_ref, after_ref, before_ref,
+    sol_ref, mat_ref, low_ref, high_ref, beside_ref, near_ref, far_ref,
     w1_ref, w2_ref, xc_ref, squeeze_ref, spread_ref,
     out_ref, ends_ref, xmat_ref, late_ref,
-    pieces, compact, xfix, hot_ref, rhs, far, fix, fixed, light, fixes, middle, sems, *scratch,
+    pieces, compact, xfix, hot_ref, rhs, far, fix, fixed, light, fixes, middle, sems,
 ):
     cells = sol_ref.shape[1]
     half = low_ref.shape[1]
     nodes = sol_ref.shape[2]
     in_low = lane_ids(SUB) < HALF
     all_low = lane_ids(cells) < HALF
+    in_first = lane_ids(cells) % HALF < HALF // 2
     side = jnp.where(in_low, 0.25, -0.25)
 
     def integral(f, r, count, t):
@@ -383,7 +408,8 @@
         compact[at, :] = jnp.dot(pieces[at, :], squeeze_ref[...], preferred_element_type=jnp.float32)
     light[...] = 1.0 / mat_ref[0]
 
-    here = near_ref[...] % cells
+    here = beside_ref[...] % cells
+    odd = odd_device()
     for k in range(2):
         direction = k + 1
         plus = hot_back(here[2 * direction : 2 * direction + 1])
@@ -418,10 +444,11 @@
                 fix[pl.ds(f * cells + r, SUB), span(k)] = value
     for f in range(9):
         at = pl.ds(f * cells, cells)
-        for k in range(2):
-            high, low = split(fix[at, span(k)])
-            fixed[at, span(k)] = high
-            fixed[at, span(k + 2)] = low
+        along, across = fix[at, span(0)], fix[at, span(1)]
+        for k, value in enumerate((jnp.where(in_first, along, across), jnp.where(in_first, across, along))):
+            high, low = split(value)
+            fixed[at, span(2 * k)] = high
+            fixed[at, span(2 * k + 1)] = low
 
     plus, minus = here[1:2], here[0:1]
     plus, minus = hot(plus, 0, cells), hot(minus, 0, cells)
@@ -434,11 +461,11 @@
     hot_ref[2, :, 2 * LANES : 3 * LANES] = late
     hot_ref[2, :, 3 * LANES : 4 * LANES] = late
     for f in range(9):
-        high, low = split(unpack_faces(after_ref[f], before_ref[f]))
+        high, low = split(unpack_faces(*got_faces(odd, near_ref, far_ref, f)))
         rhs[2, 0:LANES, span(f)] = high
         rhs[2, LANES : 2 * LANES, span(f)] = low
     for k, f in ((0, 10), (2, 9)):
-        high, low = split(unpack_faces(after_ref[f], before_ref[f]))
+        high, low = split(unpack_faces(*got_faces(odd, near_ref, far_ref, f)))
         rhs[2, k * LANES : (k + 1) * LANES, span(9)] = high
         rhs[2, (k + 1) * LANES : (k + 2) * LANES, span(9)] = low
     far[2, :, : 9 * LANES] = jnp.dot(
@@ -460,9 +487,9 @@
         for i, value in enumerate((lame, shear, weight, speed)):
             xmat_ref[i, at, :] = value
 
-    for f in range(0, 9, 3):
-        at = pl.ds(f * cells, 3 * cells)
-        fixes[at, :] = jnp.dot(fixed[at, :], spread_ref[...], preferred_element_type=jnp.float32)
+    for k in range(2):
+        at = slice(2 * k * LANES, 2 * (k + 1) * LANES)
+        fixes[:, at] = jnp.dot(fixed[:, at], spread_ref[at, :], preferred_element_type=jnp.float32)
 
     def split_rows(f, r, count, t):
         at = pl.ds(f * cells + r, count)
@@ -492,16 +519,17 @@
         for i, start in enumerate(range(0, cells, half))
     ]
     tabs = (w1_ref, w2_ref, xc_ref)
-    apply_operator(integral, split_rows, material, tabs, scratch, cells, lambda r: None, emit)
+    apply_operator(integral, split_rows, material, tabs, cells, half, lambda r: None, emit)
     for copy in stores:
         copy.wait()
 
 
-def finish_kernel(done_ref, ends_ref, after_ref, before_ref, xmat_ref, late_ref, out_ref, ends, rhs, far, sems):
+def finish_kernel(done_ref, ends_ref, near_ref, far_ref, xmat_ref, late_ref, out_ref, ends, rhs, far, sems):
     del done_ref
     cells = ends.shape[2]
+    odd = odd_device()
     for f in range(9):
-        high, low = split(unpack_faces(after_ref[f], before_ref[f]))
+        high, low = split(unpack_faces(*got_faces(odd, near_ref, far_ref, f)))
         rhs[0:LANES, span(f)] = high
         rhs[LANES : 2 * LANES, span(f)] = low
     for f in range(0, 9, 3):
@@ -529,24 +557,15 @@
         copy.wait()
 
 
-def shifted(value, axis, by):
-    peers = lax.axis_size(axis)
-    return lax.ppermute(value, axis, [(i, (i + by) % peers) for i in range(peers)])
+def exchange(near, far):
+    peers = lax.axis_size("space")
+    got_near = lax.ppermute(near, "space", [(i, i + (-1 if i % 2 else 1)) for i in range(peers)])
+    got_far = lax.ppermute(far, "space", [(i, (i + (1 if i % 2 else -1)) % peers) for i in range(peers)])
+    return got_near, got_far
 
 
 def f32(*shape):
     return jax.ShapeDtypeStruct(shape, jnp.float32)
-
-
-def operator_scratch(rows):
-    return [
-        pltpu.VMEM((len(both_yz) * TILES * rows, 3 * LANES), jnp.bfloat16),
-        pltpu.VMEM((len(pairs_yz) * TILES * rows, 6 * LANES), jnp.bfloat16),
-        pltpu.VMEM((len(both_yz) * TILES * rows, 2 * LANES), jnp.float32),
-        pltpu.VMEM((len(pairs_yz) * TILES * rows, 2 * LANES), jnp.float32),
-        pltpu.VMEM((len(along_x), rows, TILES * LANES), jnp.float32),
-        pltpu.VMEM((len(along_x), rows, TILES * LANES), jnp.float32),
-    ]
 
 
 def on_device(solution, material, neighbours, refine_count):
@@ -556,39 +575,34 @@
     early_shape, late_shape = (11, rows // 2, LANES), (9, rows // 2, LANES)
     in_vmem = pl.BlockSpec(memory_space=pltpu.VMEM)
     in_hbm = pl.BlockSpec(memory_space=pltpu.HBM)
-    in_smem = pl.BlockSpec(memory_space=pltpu.SMEM)
-    operator = operator_scratch(rows // 2) * 2
 
     sources = (solution, material) + tables() + face_tables()
-    *loaded, high, end, start = pl.pallas_call(
+    *loaded, high, near, far = pl.pallas_call(
         early_kernel,
         in_specs=[in_hbm] * LOADED,
         out_specs=[in_vmem] * (LOADED + 3),
         out_shape=[pltpu.VMEM(x.shape, x.dtype) for x in sources]
         + [pltpu.VMEM((9, rows, nodes), jnp.float32), f32(*early_shape), f32(*early_shape)],
-        scratch_shapes=[pltpu.SemaphoreType.DMA((LOADED + 2,))] + operator,
+        scratch_shapes=[pltpu.SemaphoreType.DMA((LOADED + 2,))],
         compiler_params=params(20),
         name="early",
     )(*[pltpu.with_memory_space_constraint(x, pltpu.HBM) for x in sources])
     sol, mat, w1, w2, xc, squeeze, spread = loaded
-    early_after = shifted(end, "space", -1)
-    early_before = shifted(start, "space", 1)
-
-    low, end, start = pl.pallas_call(
+    early_near, early_far = exchange(near, far)
+
+    low, near, far = pl.pallas_call(
         refined_kernel,
-        in_specs=[in_smem] + [in_vmem] * 5,
+        in_specs=[in_vmem] * 6,
         out_specs=[in_vmem] * 3,
         out_shape=[pltpu.VMEM((9, rows, nodes), jnp.float32), f32(*late_shape), f32(*late_shape)],
         scratch_shapes=[
             pltpu.VMEM((9, rows, nodes), jnp.float32),
             pltpu.VMEM((rows, nodes), jnp.float32),
-        ]
-        + operator,
+        ],
         compiler_params=params(20),
         name="refined",
     )(refine_count, sol, mat, w1, w2, xc)
-    late_after = shifted(end, "space", -1)
-    late_before = shifted(start, "space", 1)
+    late_near, late_far = exchange(near, far)
 
     done, ends, xmat, late_hot = pl.pallas_call(
         correct_kernel,
@@ -613,11 +627,10 @@
             pltpu.VMEM((9 * cells, nodes), jnp.float32),
             pltpu.VMEM((9, cells, nodes - 2 * LANES), jnp.float32),
             pltpu.SemaphoreType.DMA((2,)),
-        ]
-        + operator_scratch(rows) * 2,
+        ],
         compiler_params=params(40),
         name="correct",
-    )(sol, mat, low, high, neighbours, early_after, early_before, w1, w2, xc, squeeze, spread)
+    )(sol, mat, low, high, neighbours, early_near, early_far, w1, w2, xc, squeeze, spread)
 
     return pl.pallas_call(
         finish_kernel,
@@ -633,7 +646,7 @@
         input_output_aliases={0: 0},
         compiler_params=params(8),
         name="finish",
-    )(done, ends, late_after, late_before, xmat, late_hot)
+    )(done, ends, late_near, late_far, xmat, late_hot)
 
 
 def solution(mesh):

time: 25.4 us -> 22.3 us (0.88)
  Pallas kernels: 18.4 us -> 15.8 us
  starting transfers between devices: 6.09 us -> 4.78 us
  waiting for transfers between devices: 0.01 us -> 0.86 us
    pallas_call x1, Pallas kernels: 7.99 us -> 6.41 us  [on_device(): pl.pallas_call(refined_kernel, in_specs=[in_vmem] * 6, out_specs=[in_vmem...]
    ppermute x4, starting transfers between devices: 6.09 us -> 4.78 us  [the longest x2 4.19 us: exchange(): lax.ppermute(far, 'space', [(i, (i + (1 if i % 2 else -1)) % peers) for i...]
    ppermute x4, waiting for transfers between devices: 0.01 us -> 0.86 us  [the longest x2 0.86 us: exchange(): lax.ppermute(far, 'space', [(i, (i + (1 if i % 2 else -1)) % peers) for i...]
    pallas_call x1, Pallas kernels: 5.99 us -> 5.24 us  [on_device(): pl.pallas_call(correct_kernel, in_specs=[in_vmem] * 12, out_specs=[in_hbm...]
    pallas_call x1, Pallas kernels: 2.98 us -> 2.68 us  [on_device(): pl.pallas_call(early_kernel, in_specs=[in_hbm] * LOADED, out_specs=[in_vm...]
  transfers between devices with their start and end apart: 4 -> 4, of which waited for: 0 -> 1; matrix products, arithmetic and copies ran while one was open for 0% -> 0% of each run, Pallas kernels for 55% -> 53%
where the time goes in v3:
time: 22.3 us; the launch traced here: 22.1 us
  Pallas kernels  15.8 us (71%)
  starting transfers between devices  4.78 us (21%)
  waiting for transfers between devices  0.86 us (4%)
  between operations  0.71 us (3%)
    pallas_call x1, Pallas kernels, on_device(): pl.pallas_call(refined_kernel, in_specs=[in_vmem] * 6, out_specs=[in_vmem...  6.41 us
    pallas_call x1, Pallas kernels, on_device(): pl.pallas_call(correct_kernel, in_specs=[in_vmem] * 12, out_specs=[in_hbm...  5.24 us
    ppermute x2, starting transfers between devices, exchange(): lax.ppermute(far, 'space', [(i, (i + (1 if i % 2 else -1)) % peers) for i...  4.19 us
    pallas_call x1, Pallas kernels, on_device(): pl.pallas_call(early_kernel, in_specs=[in_hbm] * LOADED, out_specs=[in_vm...  2.68 us
    pallas_call x1, Pallas kernels, on_device(): pl.pallas_call(finish_kernel, in_specs=[in_hbm] + [in_vmem] * 5, out_spec...  1.45 us
    ppermute x2, waiting for transfers between devices, exchange(): lax.ppermute(far, 'space', [(i, (i + (1 if i % 2 else -1)) % peers) for i...  0.86 us
    ppermute x2, starting transfers between devices, exchange(): lax.ppermute(near, 'space', [(i, i + (-1 if i % 2 else 1)) for i in range...  0.59 us
  transfers between devices with their start and end apart: 4, of which 1 were waited for; matrix products, arithmetic and copies ran while one was open for 0% of the time, Pallas kernels for 53%

profile of v3, /device:TPU:0, one launch (start us, length us, event | category | flops | bytes accessed | tf_op | source)
XLA Modules:
  0.0 22.1 jit_solution(6841476100839930240)
XLA Ops:
  0.0 2.7 %early.1 = (f32[9,128,512]{2,1,0:T(8,128)S(1)}, f32[3,128,512]{2,1,0:T(8,128)S(1)}, bf16[384,256]{1,0:T(8,128)(2,1)S(1)}, bf16[768,256]{1,0:T(8,128)(2,1)S(1)}, ...) custom-call(f32[9,128,512]{2,1,0:T(8,128)} %refs_0_.1, ...), custom_call_target="tpu_custom_call" | custom-call | tf_op jit(solution)/shard_map/early/pallas_call | solution.py:580
  2.7 0.0 copy-start
  2.7 0.5 %collective-permute-start = (f32[11,32,128]{2,1,0:T(8,128)S(1)}, f32[11,32,128]{2,1,0:T(8,128)S(1)}, u32[]{:S(2)}, u32[]{:S(2)}) collective-permute-start(f32[11,32,128]{2,1,0:T(8,128)S(1)} %get-tuple-element.29), channel_id=1, source_target_pairs={{0,4},{4,0},{8,12},{12,8},{16,20},{20,16},{24,28},{28,24},{1,5},{5... | collective-permute-start | bytes 540680 | tf_op jit(solution)/shard_map/ppermute | solution.py:562
  3.2 3.6 %collective-permute-start.1 = (f32[11,32,128]{2,1,0:T(8,128)S(1)}, f32[11,32,128]{2,1,0:T(8,128)S(1)}, u32[]{:S(2)}, u32[]{:S(2)}) collective-permute-start(f32[11,32,128]{2,1,0:T(8,128)S(1)} %get-tuple-element.30), channel_id=1, source_target_pairs={{0,28},{4,8},{8,4},{12,16},{16,12},{20,24},{24,20},{28,0},{1,29},{... | collective-permute-start | bytes 540680 | tf_op jit(solution)/shard_map/ppermute | solution.py:563
  7.4 6.4 %refined.1 = (f32[9,64,512]{2,1,0:T(8,128)S(1)}, f32[9,32,128]{2,1,0:T(8,128)S(1)}, f32[9,32,128]{2,1,0:T(8,128)S(1)}) custom-call(s32[1,1]{1,0:T(1,128)S(6)} %copy.12.count_ref, f32[9,128,512]{2,1,0:T(8,128)S(1)} %get-tuple-element.22.sol_ref, f32[3,128,512]{2,1,0:T(8,128)S(1)} %get-tuple-element.23.mat_ref, bf16[384,256]{1,0:T(8,128)(2,1)S(1)} %get-tuple-element.24.w1_ref, ...), custom_call_target="tpu_custom_call" | custom-call | tf_op jit(solution)/shard_map/refined/pallas_call | solution.py:593
  13.8 0.1 collective-permute-start.2
  13.9 0.6 %collective-permute-start.3 = (f32[9,32,128]{2,1,0:T(8,128)S(1)}, f32[9,32,128]{2,1,0:T(8,128)S(1)}, u32[]{:S(2)}, u32[]{:S(2)}) collective-permute-start(f32[9,32,128]{2,1,0:T(8,128)S(1)} %get-tuple-element.36), channel_id=1, source_target_pairs={{0,28},{4,8},{8,4},{12,16},{16,12},{20,24},{24,20},{28,0},{1,29},{... | collective-permute-start | bytes 442376 | tf_op jit(solution)/shard_map/ppermute | solution.py:563
  14.6 0.0 collective-permute-done.near_ref
  14.6 0.0 collective-permute-done.1.far_ref
  14.6 0.0 copy-done
  14.6 5.2 %correct.1 = (f32[9,128,512]{2,1,0:T(8,128)}, f32[2,9,128,128]{3,2,1,0:T(8,128)S(1)}, f32[4,128,128]{2,1,0:T(8,128)S(1)}, bf16[128,256]{1,0:T(8,128)(2,1)S(1)}) custom-call(f32[9,128,512]{2,1,0:T(8,128)S(1)} %get-tuple-element.22.sol_ref, f32[3,128,512]{2,1,0:T(8,128)S(1)} %get-tuple-element.23.mat_ref, f32[9,64,512]{2,1,0:T(8,128)S(1)} %get-tuple-element.27.low_ref, ...), custom_call_target="tpu_custom_call" | custom-call | tf_op jit(solution)/shard_map/correct/pallas_call | solution.py:607
  19.8 0.0 collective-permute-done.2.near_ref
  19.8 0.9 %collective-permute-done.3.far_ref = f32[9,32,128]{2,1,0:T(8,128)S(1)} collective-permute-done((f32[9,32,128]{2,1,0:T(8,128)S(1)}, f32[9,32,128]{2,1,0:T(8,128)S(1)}, u32[]{:S(2)}, u32[]{:S(2)}) %collective-permute-start.3) | collective-permute-done | bytes 147488 | tf_op jit(solution)/shard_map/ppermute | solution.py:563
  20.7 1.4 %finish.1 = f32[9,128,512]{2,1,0:T(8,128)} custom-call(f32[9,128,512]{2,1,0:T(8,128)} %get-tuple-element.33.done_ref, f32[2,9,128,128]{3,2,1,0:T(8,128)S(1)} %get-tuple-element.34.ends_ref, f32[9,32,128]{2,1,0:T(8,128)S(1)} %collective-permute-done.2.near_ref, f32[9,32,128]{2,1,0:T(8,128)S(1)} %collective-permute-done.3.far_ref, ...), custom_call_target="tpu_custom_call", output_to_operand_aliasing={{}: (0, {})} | custom-call | tf_op jit(solution)/shard_map/finish/pallas_call | solution.py:635
Async XLA Ops:
  2.7 11.9 %copy-start = (s32[6,128]{1,0:T(8,128)S(1)}, s32[6,128]{1,0:T(8,128)}, u32[]{:S(2)}) copy-start(s32[6,128]{1,0:T(8,128)} %beside_ref.1) | copy-start | bytes 9220
  2.7 11.9 %collective-permute-start = (f32[11,32,128]{2,1,0:T(8,128)S(1)}, f32[11,32,128]{2,1,0:T(8,128)S(1)}, u32[]{:S(2)}, u32[]{:S(2)}) collective-permute-start(f32[11,32,128]{2,1,0:T(8,128)S(1)} %get-tuple-element.29), channel_id=1, source_target_pairs={{0,4},{4,0},{8,12},{12,8},{16,20},{20,16},{24,28},{28,24},{1,5},{5... | collective-permute-start | bytes 540680 | tf_op jit(solution)/shard_map/ppermute | solution.py:562
  3.2 11.3 %collective-permute-start.1 = (f32[11,32,128]{2,1,0:T(8,128)S(1)}, f32[11,32,128]{2,1,0:T(8,128)S(1)}, u32[]{:S(2)}, u32[]{:S(2)}) collective-permute-start(f32[11,32,128]{2,1,0:T(8,128)S(1)} %get-tuple-element.30), channel_id=1, source_target_pairs={{0,28},{4,8},{8,4},{12,16},{16,12},{20,24},{24,20},{28,0},{1,29},{... | collective-permute-start | bytes 540680 | tf_op jit(solution)/shard_map/ppermute | solution.py:563
  13.8 6.0 %collective-permute-start.2 = (f32[9,32,128]{2,1,0:T(8,128)S(1)}, f32[9,32,128]{2,1,0:T(8,128)S(1)}, u32[]{:S(2)}, u32[]{:S(2)}) collective-permute-start(f32[9,32,128]{2,1,0:T(8,128)S(1)} %get-tuple-element.35), channel_id=1, source_target_pairs={{0,4},{4,0},{8,12},{12,8},{16,20},{20,16},{24,28},{28,24},{1,5},{5... | collective-permute-start | bytes 442376 | tf_op jit(solution)/shard_map/ppermute | solution.py:562
  13.9 6.8 %collective-permute-start.3 = (f32[9,32,128]{2,1,0:T(8,128)S(1)}, f32[9,32,128]{2,1,0:T(8,128)S(1)}, u32[]{:S(2)}, u32[]{:S(2)}) collective-permute-start(f32[9,32,128]{2,1,0:T(8,128)S(1)} %get-tuple-element.36), channel_id=1, source_target_pairs={{0,28},{4,8},{8,4},{12,16},{16,12},{20,24},{24,20},{28,0},{1,29},{... | collective-permute-start | bytes 442376 | tf_op jit(solution)/shard_map/ppermute | solution.py:563
